TPU v7x, 512 devices: a whole 4x8x8 slice. The times are simulated.
512 devices in a mesh: row: 64 (over x, z, core), col: 8 (over y).
Axes of the slice: x: 4, y: 8, z: 8, core: 2. Of those that a mesh axis runs over, the one named last changes fastest.
Arguments:
- src_points: bfloat16 [262144, 64], P('row'), may hold values from -36 to 36
- tgt_points: bfloat16 [65536, 64], P('col'), may hold values from -36 to 36
- src_counts: int32 [1024], P('row'), may hold values from 64 to 256, as said below
- tgt_counts: int32 [256], P('col'), may hold values from 64 to 256, as said below
- tile_list: int32 [64, 8, 48, 2], P('row', 'col'), may hold values from 0 to 31, as said below
- tile_count: int32 [64, 8], P('row', 'col'), may hold values from 16 to 48, as said below
Outputs:
- src_potential: float32 [262144], P('row')
- tgt_potential: float32 [65536], P('col')
Inputs may be any that keep to these rules, and one draw needn't show every extreme that they name: The first src_counts[b] slots of source block b are real; some block is full. The first tgt_counts[b] slots of target block b are real; some block is full. `tile_list`: entries (k, l) with k < 16 and l < 32; the pairs of one device differ; slot k < 16 of every device holds source block k; every target block is in a live slot of some device. `tile_count`: some device has all 48 slots live.
All inputs are finite; a program needn't handle non-finite values.
Results may differ from a plain program's by a relative error of at most 0.0003.
Values sent between devices are 32-bit elements; how exact they have to be, the bound alone decides.
No kernel may reach another device: no remote copies, remote signals or barrier semaphores. Data moves between devices by JAX's collectives and lax.ppermute only.
A program may use at most 64 MiB of HBM per device.

v0:
```python
import jax
import jax.numpy as jnp
from jax import lax
from jax.sharding import PartitionSpec as P

BLOCK = 256
ITERS = 3


epsilon = 0.05
very_low = -1e30


def tile_costs(src_blocks, tgt_blocks, src_norms, tgt_norms, rows, cols):
    picked_src = src_blocks[rows]
    picked_tgt = tgt_blocks[cols]
    dots = jnp.einsum("tid,tjd->tij", picked_src, picked_tgt, preferred_element_type=jnp.float32)
    return (
        src_norms[rows][:, :, None] + tgt_norms[cols][:, None, :] - 2.0 * dots
    ) / picked_src.shape[-1]


def fold_tiles(peak, mass, top, total, owner, used):
    member = (owner[:, None] == jnp.arange(peak.shape[0], dtype=jnp.int32)[None, :]) & used[:, None]
    top = jnp.where(used[:, None], top, very_low)
    candidate = jnp.max(jnp.where(member[:, :, None], top[:, None, :], very_low), axis=0)
    newpeak = jnp.maximum(peak, candidate)
    added = jnp.sum(
        jnp.where(
            member[:, :, None], total[:, None, :] * jnp.exp(top[:, None, :] - newpeak[None]), 0.0
        ),
        axis=0,
    )
    return (newpeak, mass * jnp.exp(peak - newpeak) + added)


def on_device(src_points, tgt_points, src_counts, tgt_counts, tile_list, tile_count):
    width = BLOCK
    src_nblk = src_counts.shape[0]
    tgt_nblk = tgt_counts.shape[0]
    src_blocks = src_points.reshape(src_nblk, width, -1)
    tgt_blocks = tgt_points.reshape(tgt_nblk, width, -1)
    src_norms = jnp.sum(jnp.square(src_blocks.astype(jnp.float32)), axis=-1)
    tgt_norms = jnp.sum(jnp.square(tgt_blocks.astype(jnp.float32)), axis=-1)
    positions = jnp.arange(width, dtype=jnp.int32)
    src_valid = positions[None, :] < src_counts[:, None]
    tgt_valid = positions[None, :] < tgt_counts[:, None]
    pairs = tile_list.reshape(-1, 2)
    live = tile_count.reshape(())
    rounds = (live + 7) // 8
    src_local = jnp.sum(src_counts).astype(jnp.float32)
    tgt_local = jnp.sum(tgt_counts).astype(jnp.float32)
    src_total = lax.psum(src_local, "row")
    tgt_total = lax.psum(tgt_local, "col")
    log_src = jnp.log(src_total)
    log_tgt = jnp.log(tgt_total)

    def sweep(potential, along_rows):
        count = src_nblk if along_rows else tgt_nblk
        start = (
            jnp.full((count, width), very_low, jnp.float32),
            jnp.zeros((count, width), jnp.float32),
        )

        def group(turn, carry):
            picked = lax.dynamic_slice_in_dim(pairs, turn * 8, 8, 0)
            rows = picked[:, 0]
            cols = picked[:, 1]
            used = turn * 8 + jnp.arange(8, dtype=jnp.int32) < live
            costs = tile_costs(src_blocks, tgt_blocks, src_norms, tgt_norms, rows, cols)
            if along_rows:
                keep = tgt_valid[cols][:, None, :] & used[:, None, None]
                scores = jnp.where(keep, (potential[cols][:, None, :] - costs) / epsilon, very_low)
                top = jnp.max(scores, axis=2)
                total = jnp.sum(jnp.exp(scores - top[:, :, None]), axis=2)
                owner = rows
            else:
                keep = src_valid[rows][:, :, None] & used[:, None, None]
                scores = jnp.where(keep, (potential[rows][:, :, None] - costs) / epsilon, very_low)
                top = jnp.max(scores, axis=1)
                total = jnp.sum(jnp.exp(scores - top[:, None, :]), axis=1)
                owner = cols
            return fold_tiles(carry[0], carry[1], top, total, owner, used)

        return lax.fori_loop(0, rounds, group, start)

    tgt_pot = jnp.zeros((tgt_nblk, width), jnp.float32)
    src_pot = jnp.zeros((src_nblk, width), jnp.float32)
    for step in range(ITERS):
        peak, mass = sweep(tgt_pot, True)
        whole_peak = lax.pmax(peak, "col")
        whole_mass = lax.psum(mass * jnp.exp(peak - whole_peak), "col")
        src_pot = jnp.where(src_valid, -epsilon * (log_src + whole_peak + jnp.log(whole_mass)), 0.0)
        peak, mass = sweep(src_pot, False)
        whole_peak = lax.pmax(peak, "row")
        whole_mass = lax.psum(mass * jnp.exp(peak - whole_peak), "row")
        tgt_pot = jnp.where(tgt_valid, -epsilon * (log_tgt + whole_peak + jnp.log(whole_mass)), 0.0)
    return (src_pot.reshape(-1), tgt_pot.reshape(-1))


def solution(mesh):
    return jax.shard_map(
        on_device,
        mesh=mesh,
        in_specs=(
            P("row", None),
            P("col", None),
            P("row"),
            P("col"),
            P("row", "col", None, None),
            P("row", "col"),
        ),
        out_specs=(P("row"), P("col")),
        check_vma=False,
    )
```

profile of v0, /device:TPU:1, one launch (start us, length us, event | category | flops | bytes accessed | tf_op | source)
XLA Modules:
  0.0 2071.3 jit_solution(4954691511802508453)
XLA Ops:
  1.3 2.0 copy.35
  7.6 17.8 while.78
  13.7 2.2 fusion.74
  22.6 2.2 fusion.74
  25.4 58.3 %pmax.42 = f32[16,256]{1,0:T(8,128)S(1)} all-reduce(f32[16,256]{1,0:T(8,128)S(1)} %get-tuple-element.381), channel_id=1, replica_groups=mesh['row'=64,'col'=8] {'col'}, use_global_device_ids=true, to_apply=%region_12.13 | all-reduce | flops 4096 | bytes 32768 | tf_op jit(solution)/shard_map/pmax | solution.py:91
  85.0 21.1 %all-reduce = (f32[16,256]{1,0:T(8,128)S(1)}, f32[]{:T(128)}) all-reduce(f32[16,256]{1,0:T(8,128)S(1)} %exponential_multiply_fusion.5, f32[]{:T(128)S(6)} %convert_element_type.15), channel_id=1, replica_groups=mesh['row'=64,'col'=8] {'col'}, use_global_device_ids=true, to_apply=%region_13.14 | all-reduce | flops 4097 | bytes 32776 | tf_op jit(solution)/shard_map/psum | solution.py:92
  107.4 140.4 %psum.56 = f32[]{:T(128)} all-reduce(f32[]{:T(128)S(6)} %convert_element_type.14), channel_id=1, replica_groups=mesh['row'=64,'col'=8] {'row'}, use_global_device_ids=true, to_apply=%region_1.0 | all-reduce | flops 1 | bytes 8 | tf_op jit(solution)/shard_map/psum | solution.py:53
  248.5 17.8 while.79
  254.5 2.2 fusion.78
  263.4 2.2 fusion.78
  266.4 266.9 %pmax.43 = f32[32,256]{1,0:T(8,128)S(1)} all-reduce(f32[32,256]{1,0:T(8,128)S(1)} %get-tuple-element.383), channel_id=1, replica_groups=mesh['row'=64,'col'=8] {'row'}, use_global_device_ids=true, to_apply=%region_20.21 | all-reduce | flops 8192 | bytes 65536 | tf_op jit(solution)/shard_map/pmax | solution.py:95
  533.2 246.1 %psum.59 = f32[32,256]{1,0:T(8,128)S(1)} all-reduce(f32[32,256]{1,0:T(8,128)S(1)} %exponential_multiply_fusion.2), channel_id=1, replica_groups=mesh['row'=64,'col'=8] {'row'}, use_global_device_ids=true, to_apply=%region_21.22 | all-reduce | flops 8192 | bytes 65536 | tf_op jit(solution)/shard_map/psum | solution.py:96
  780.2 17.7 while.80
  786.2 2.2 fusion.82
  795.1 2.2 fusion.82
  798.0 63.8 %pmax.44 = f32[16,256]{1,0:T(8,128)S(1)} all-reduce(f32[16,256]{1,0:T(8,128)S(1)} %get-tuple-element.385), channel_id=1, replica_groups=mesh['row'=64,'col'=8] {'col'}, use_global_device_ids=true, to_apply=%region_28.29 | all-reduce | flops 4096 | bytes 32768 | tf_op jit(solution)/shard_map/pmax | solution.py:91
  861.7 21.5 %psum.60 = f32[16,256]{1,0:T(8,128)S(1)} all-reduce(f32[16,256]{1,0:T(8,128)S(1)} %exponential_multiply_fusion.4), channel_id=1, replica_groups=mesh['row'=64,'col'=8] {'col'}, use_global_device_ids=true, to_apply=%region_29.30 | all-reduce | flops 4096 | bytes 32768 | tf_op jit(solution)/shard_map/psum | solution.py:92
  883.3 17.8 while.81
  889.3 2.2 fusion.86
  898.3 2.2 fusion.86
  901.2 272.1 %pmax.45 = f32[32,256]{1,0:T(8,128)S(1)} all-reduce(f32[32,256]{1,0:T(8,128)S(1)} %get-tuple-element.387), channel_id=1, replica_groups=mesh['row'=64,'col'=8] {'row'}, use_global_device_ids=true, to_apply=%region_36.37 | all-reduce | flops 8192 | bytes 65536 | tf_op jit(solution)/shard_map/pmax | solution.py:95
  1173.3 246.1 %psum.61 = f32[32,256]{1,0:T(8,128)S(1)} all-reduce(f32[32,256]{1,0:T(8,128)S(1)} %exponential_multiply_fusion.1), channel_id=1, replica_groups=mesh['row'=64,'col'=8] {'row'}, use_global_device_ids=true, to_apply=%region_37.38 | all-reduce | flops 8192 | bytes 65536 | tf_op jit(solution)/shard_map/psum | solution.py:96
  1419.5 17.7 while.82
  1425.5 2.2 fusion.90
  1434.4 2.2 fusion.90
  1437.2 75.7 %pmax.46 = f32[16,256]{1,0:T(8,128)S(1)} all-reduce(f32[16,256]{1,0:T(8,128)S(1)} %get-tuple-element.389), channel_id=1, replica_groups=mesh['row'=64,'col'=8] {'col'}, use_global_device_ids=true, to_apply=%region_44.45 | all-reduce | flops 4096 | bytes 32768 | tf_op jit(solution)/shard_map/pmax | solution.py:91
  1512.9 20.1 psum.62
  1533.1 17.8 while.83
  1539.1 2.2 fusion.94
  1548.0 2.2 fusion.94
  1550.9 272.9 %pmax.47 = f32[32,256]{1,0:T(8,128)S(1)} all-reduce(f32[32,256]{1,0:T(8,128)S(1)} %get-tuple-element.391), channel_id=1, replica_groups=mesh['row'=64,'col'=8] {'row'}, use_global_device_ids=true, to_apply=%region_52.53 | all-reduce | flops 8192 | bytes 65536 | tf_op jit(solution)/shard_map/pmax | solution.py:95
  1823.8 246.1 %psum.63 = f32[32,256]{1,0:T(8,128)S(1)} all-reduce(f32[32,256]{1,0:T(8,128)S(1)} %exponential_multiply_fusion), channel_id=1, replica_groups=mesh['row'=64,'col'=8] {'row'}, use_global_device_ids=true, to_apply=%region_53.54 | all-reduce | flops 8192 | bytes 65536 | tf_op jit(solution)/shard_map/psum | solution.py:96
  (281 shorter events, 86.9 us)
Async XLA Ops:
  3.3 4.3 copy-start
  3.3 4.3 copy-start.2
  7.6 98.4 %copy-start.1 = (s32[16]{0:T(128)S(1)}, s32[16]{0:T(128)}, u32[]{:S(2)}) copy-start(s32[16]{0:T(128)} %param.20) | copy-start | bytes 196
where the time goes:
time: 2100 us; the launch traced here: 2070 us
  blocking collectives  1950 us (93%)
  local copies, waits for them, and re-layouts  66.8 us (3%)
  matrix products  26 us (1%)
  other arithmetic  22.2 us (1%)
    pmax x3, blocking collectives, on_device(): whole_peak = lax.pmax(peak, 'row')  812 us
    psum x3, blocking collectives, on_device(): whole_mass = lax.psum(mass * jnp.exp(peak - whole_peak), 'row')  738 us
    pmax x3, blocking collectives, on_device(): whole_peak = lax.pmax(peak, 'col')  198 us
    psum x1, blocking collectives, on_device(): src_total = lax.psum(src_local, 'row')  140 us
    psum x3, blocking collectives, on_device(): whole_mass = lax.psum(mass * jnp.exp(peak - whole_peak), 'col')  62.7 us

commit v1 on v0

v1 whole, which is shorter than its diff:
```python
import functools
import math

import jax
import jax.numpy as jnp
from jax import lax
from jax.experimental import pallas as pl
from jax.experimental.pallas import tpu as pltpu
from jax.sharding import Mesh, PartitionSpec as P

BLOCK = 256
ITERS = 3
LANES = 128

epsilon = 0.05
very_low = -1e30
DIM = 64
SCALE = 2.0 / (DIM * epsilon) * math.log2(math.e)
INV_SCALE = 1.0 / SCALE


def merged(parts):
    top = jnp.max(parts, axis=0)
    total = jnp.sum(jnp.exp2((parts - top[None]) * SCALE), axis=0)
    return top + jnp.log2(total) * INV_SCALE


def sweep_kernel(side, live_ref, pairs_ref, bias_ref, red_ref, col_ref, out_ref, peak, mass, ta, tb):
    nred = bias_ref.shape[0]
    ncol = out_ref.shape[0]
    bias = bias_ref[...]
    hi = bias.astype(jnp.bfloat16).astype(jnp.float32)
    rest = bias - hi
    mid = rest.astype(jnp.bfloat16).astype(jnp.float32)
    low = rest - mid
    blank = jnp.zeros((DIM, BLOCK), jnp.float32)
    half = DIM // 2
    if nred < half:
        pad = jnp.zeros((half - nred, BLOCK), jnp.float32)
        hi, mid, low = (jnp.concatenate([v, pad], axis=0) for v in (hi, mid, low))
    ta[...] = jnp.concatenate([blank, hi, mid], axis=0).T.astype(jnp.bfloat16)
    tb[...] = jnp.concatenate([low, blank, blank[:half]], axis=0).T.astype(jnp.bfloat16)
    peak[...] = jnp.full(peak.shape, very_low, jnp.float32)
    mass[...] = jnp.zeros(mass.shape, jnp.float32)
    lane = lax.broadcasted_iota(jnp.int32, (1, LANES), 1)

    def tile(t, _):
        red = pairs_ref[2 * t + side]
        col = pairs_ref[2 * t + 1 - side]
        one_a = ((lane == DIM + red) | (lane == DIM + half + red)).astype(jnp.float32).astype(jnp.bfloat16)
        one_b = (lane == red).astype(jnp.float32).astype(jnp.bfloat16)
        lhs = red_ref[pl.ds(pl.multiple_of(red * BLOCK, BLOCK), BLOCK), :] + ta[...]
        rhs = col_ref[pl.ds(pl.multiple_of(col * BLOCK, BLOCK), BLOCK), :] + one_a
        lhs = jnp.concatenate([lhs, tb[...]], axis=1)
        rhs = jnp.concatenate([rhs, jnp.broadcast_to(one_b, (BLOCK, LANES))], axis=1)
        score = lax.dot_general(
            lhs, rhs, (((1,), (1,)), ((), ())), preferred_element_type=jnp.float32
        ).reshape(BLOCK // 8, 8, BLOCK)
        old = peak[col]
        new = jnp.maximum(old, jnp.max(score, axis=0))
        total = jnp.sum(jnp.exp2((score - new[None]) * SCALE), axis=0)
        mass[col] = mass[col] * jnp.exp2((old - new) * SCALE) + total
        peak[col] = new
        return 0

    lax.fori_loop(0, live_ref[0], tile, 0)
    top = jnp.max(peak[...], axis=1, keepdims=True)
    total = jnp.sum(mass[...] * jnp.exp2((peak[...] - top) * SCALE), axis=1)
    top = top.reshape(ncol, BLOCK)
    used = total > 0.0
    out_ref[...] = jnp.where(used, top + jnp.log2(jnp.where(used, total, 1.0)) * INV_SCALE, very_low)


def sweep(side, live, pairs, bias, red, col):
    ncol = col.shape[0] // BLOCK
    smem = pl.BlockSpec(memory_space=pltpu.SMEM)
    vmem = pl.BlockSpec(memory_space=pltpu.VMEM)
    return pl.pallas_call(
        functools.partial(sweep_kernel, side),
        out_shape=jax.ShapeDtypeStruct((ncol, BLOCK), jnp.float32),
        in_specs=[smem, smem, vmem, vmem, vmem],
        out_specs=vmem,
        scratch_shapes=[
            pltpu.VMEM((ncol, 8, BLOCK), jnp.float32),
            pltpu.VMEM((ncol, 8, BLOCK), jnp.float32),
            pltpu.VMEM((BLOCK, LANES), jnp.bfloat16),
            pltpu.VMEM((BLOCK, LANES), jnp.bfloat16),
        ],
        compiler_params=pltpu.CompilerParams(vmem_limit_bytes=24 * 1024 * 1024),
    )(live, pairs, bias, red, col)


def spread(value, axes, count):
    stacked = jnp.broadcast_to(value[None], (count,) + value.shape)
    return lax.all_to_all(stacked, axes, 0, 0)


def on_device(sizes, src_points, tgt_points, src_counts, tgt_counts, tile_list, tile_count):
    src_nblk = src_counts.shape[0]
    tgt_nblk = tgt_counts.shape[0]
    nplane = sizes["x"] * sizes["z"]
    ny = sizes["y"]
    pad = ((0, 0), (0, LANES - DIM))
    src = jnp.pad(src_points, pad)
    tgt = jnp.pad(tgt_points, pad)
    src_norms = jnp.sum(jnp.square(src_points.astype(jnp.float32)), axis=-1).reshape(src_nblk, BLOCK)
    tgt_norms = jnp.sum(jnp.square(tgt_points.astype(jnp.float32)), axis=-1).reshape(tgt_nblk, BLOCK)
    positions = jnp.arange(BLOCK, dtype=jnp.int32)
    src_valid = positions[None, :] < src_counts[:, None]
    tgt_valid = positions[None, :] < tgt_counts[:, None]
    pairs = tile_list.reshape(-1)
    live = tile_count.reshape(-1)
    src_local = jnp.sum(src_counts).astype(jnp.float32)
    tgt_local = jnp.sum(tgt_counts).astype(jnp.float32)
    core = lax.axis_index("core")
    half = tgt_nblk // 2

    tgt_pot = -0.5 * tgt_norms
    for step in range(ITERS):
        bias = jnp.where(tgt_valid, tgt_pot, very_low)
        part = sweep(1, live, pairs, bias, tgt, src)
        if step == 0:
            part = jnp.concatenate([part, jnp.full((8, BLOCK), tgt_local)], axis=0)
        parts = spread(part, "y", ny)
        if step == 0:
            tgt_total = jnp.sum(parts[:, src_nblk, 0])
            parts = parts[:, :src_nblk]
        src_pot = -merged(parts)
        bias = jnp.where(src_valid, src_pot, very_low)
        part = sweep(0, live, pairs, bias, src, tgt)
        if step == 0:
            pair = lax.all_gather(jnp.concatenate([part, jnp.full((8, BLOCK), src_local)], axis=0), "core")
            mine = merged(lax.dynamic_slice_in_dim(pair, core * half, half, 1))
            both = jnp.sum(pair[:, tgt_nblk, 0])
            parts = spread(jnp.concatenate([mine, jnp.full((8, BLOCK), both)], axis=0), ("x", "z"), nplane)
            src_total = jnp.sum(parts[:, half, 0])
            parts = parts[:, :half]
        else:
            pair = lax.all_gather(part, "core")
            mine = merged(lax.dynamic_slice_in_dim(pair, core * half, half, 1))
            parts = spread(mine, ("x", "z"), nplane)
        tgt_pot = -lax.all_gather(merged(parts), "core", axis=0, tiled=True)
    log_src = jnp.log(src_total)
    log_tgt = jnp.log(tgt_total)
    src_shift = -epsilon * (ITERS * log_src - (ITERS - 1) * log_tgt)
    tgt_shift = epsilon * ITERS * (log_src - log_tgt)
    src_out = jnp.where(src_valid, src_pot * (2.0 / DIM) + src_norms * (1.0 / DIM) + src_shift, 0.0)
    tgt_out = jnp.where(tgt_valid, tgt_pot * (2.0 / DIM) + tgt_norms * (1.0 / DIM) + tgt_shift, 0.0)
    return (src_out.reshape(-1), tgt_out.reshape(-1))


def solution(mesh):
    sizes = {"x": 4, "z": 8, "core": 2, "y": mesh.shape["col"]}
    fine = Mesh(mesh.devices.reshape(tuple(sizes.values())), tuple(sizes))
    row = ("x", "z", "core")
    return jax.shard_map(
        functools.partial(on_device, sizes),
        mesh=fine,
        in_specs=(P(row, None), P("y", None), P(row), P("y"), P(row, "y", None, None), P(row, "y")),
        out_specs=(P(row), P("y")),
        check_vma=False,
    )
```

time: 2100 us -> 237 us (0.11); the launches traced: 2070 us -> 236 us
  blocking collectives: 1950 us -> 106 us
  local copies, waits for them, and re-layouts: 66.8 us -> 10.9 us
  Pallas kernels: 0 us -> 49 us
  starting transfers between devices: 0 us -> 32.1 us
  matrix products: 26 us -> 0 us
  waiting for transfers between devices: 0 us -> 24.9 us
    pmax x6 -> x0, blocking collectives: 1010 us -> none  [the longest x3 812 us: on_device(): whole_peak = lax.pmax(peak, 'row')]
    psum x7 -> x0, blocking collectives: 941 us -> none  [the longest x3 738 us: on_device(): whole_mass = lax.psum(mass * jnp.exp(peak - whole_peak), 'row')]
    all_to_all x0 -> x3, blocking collectives: none -> 75.8 us  [spread(): return lax.all_to_all(stacked, axes, 0, 0)]
    gather x72 -> x0, local copies, waits for them, and re-layouts: 61 us -> none  [the longest x12 17.1 us: tile_costs(): picked_tgt = tgt_blocks[cols]]
    pallas_call x0 -> x6, Pallas kernels: none -> 49 us  [sweep(): pl.pallas_call(functools.partial(sweep_kernel, side), out_shape=jax.Shape...]
    all_to_all x0 -> x3, starting transfers between devices: none -> 32.1 us  [spread(): return lax.all_to_all(stacked, axes, 0, 0)]
    all_gather x0 -> x6, blocking collectives: none -> 30.6 us  [the longest x3 16.4 us: on_device(): tgt_pot = -lax.all_gather(merged(parts), 'core', axis=0, tiled=True)]
    dot_general x12 -> x0, matrix products: 26 us -> none  [tile_costs(): jnp.einsum('tid,tjd->tij', picked_src, picked_tgt, preferred_element_type...]
  transfers between devices with their start and end apart: 0 -> 3, of which waited for: 0 -> 3; matrix products, arithmetic and copies ran while one was open for 0% -> 2% of each run, Pallas kernels for 0% -> 0%
where the time goes in v1:
time: 237 us; the launch traced here: 236 us
  blocking collectives  106 us (45%)
  Pallas kernels  49 us (21%)
  starting transfers between devices  32.1 us (14%)
  waiting for transfers between devices  24.9 us (11%)
  local copies, waits for them, and re-layouts  10.9 us (5%)
  other arithmetic  8.42 us (4%)
  between operations  4.31 us (2%)
    all_to_all x3, blocking collectives, spread(): return lax.all_to_all(stacked, axes, 0, 0)  75.8 us
    pallas_call x6, Pallas kernels, sweep(): pl.pallas_call(functools.partial(sweep_kernel, side), out_shape=jax.Shape...  49 us
    all_to_all x3, starting transfers between devices, spread(): return lax.all_to_all(stacked, axes, 0, 0)  32.1 us
    all_to_all x3, waiting for transfers between devices, spread(): return lax.all_to_all(stacked, axes, 0, 0)  24.9 us
    all_gather x3, blocking collectives, on_device(): tgt_pot = -lax.all_gather(merged(parts), 'core', axis=0, tiled=True)  16.4 us
    all_gather x2, blocking collectives, on_device(): pair = lax.all_gather(part, 'core')  8.04 us
    all_gather x1, blocking collectives, on_device(): lax.all_gather(jnp.concatenate([part, jnp.full((8, BLOCK), src_local)], a...  6.17 us
    unnamed x21, local copies, waits for them, and re-layouts  5.44 us
  transfers between devices with their start and end apart: 3, of which 3 were waited for; matrix products, arithmetic and copies ran while one was open for 2% of the time, Pallas kernels for 0%

profile of v1, /device:TPU:1, one launch (start us, length us, event | category | flops | bytes accessed | tf_op | source)
XLA Modules:
  0.0 236.0 jit_solution(6342584420614563291)
XLA Ops:
  0.7 2.9 %copy.25 = bf16[8192,64]{1,0:T(8,128)(2,1)} copy(bf16[8192,64]{0,1:T(8,128)(2,1)} %param.7) | data formatting | bytes 2097152 | tf_op args[1]
  3.8 1.3 copy.26
  5.2 2.1 pad.11.red_ref.col_ref
  10.2 8.1 %shard_map.77 = f32[16,256]{1,0:T(8,128)S(1)} custom-call(s32[1]{0:T(128)} %bitcast.12.live_ref, s32[96]{0:T(128)S(1)} %reshape.60.pairs_ref, f32[32,256]{1,0:T(8,128)S(1)} %fusion.bias_ref, bf16[8192,128]{1,0:T(8,128)(2,1)S(1)} %pad.11.red_ref.col_ref, bf16[4096,128]{1,0:T(8,128)(2,1)S(1)} %pad.12.col_ref.red_ref), custom_call_target="tpu_custom_call" | custom-call | tf_op jit(solution)/shard_map/pallas_call | solution.py:78
  18.4 0.7 broadcast_in_dim.31
  19.0 9.8 %all-to-all-start = ((f32[8,24,256]{2,1,0:T(8,128)}), f32[8,24,256]{2,1,0:T(8,128)S(1)}, u32[]{:S(2)}, u32[]{:S(2)}) async-start(f32[8,24,256]{2,1,0:T(8,128)} %broadcast_in_dim.31), calls=%async_computation | async-start | bytes 393216 | tf_op jit(solution)/shard_map/all_to_all | solution.py:95
  30.2 7.4 %all-to-all-done = f32[8,24,256]{2,1,0:T(8,128)S(1)} async-done(((f32[8,24,256]{2,1,0:T(8,128)}), f32[8,24,256]{2,1,0:T(8,128)S(1)}, u32[]{:S(2)}, u32[]{:S(2)}) %all-to-all-start) | async-done | bytes 196640 | tf_op jit(solution)/shard_map/all_to_all | solution.py:95
  37.7 8.2 %shard_map.78 = f32[32,256]{1,0:T(8,128)S(1)} custom-call(s32[1]{0:T(128)} %bitcast.13.live_ref, s32[96]{0:T(128)S(1)} %reshape.60.pairs_ref, f32[16,256]{1,0:T(8,128)S(1)} %negate_select_fusion.3.bias_ref, bf16[4096,128]{1,0:T(8,128)(2,1)S(1)} %pad.12.col_ref.red_ref, bf16[8192,128]{1,0:T(8,128)(2,1)S(1)} %pad.11.red_ref.col_ref), custom_call_target="tpu_custom_call" | custom-call | tf_op jit(solution)/shard_map/pallas_call | solution.py:78
  46.0 6.2 %all-gather = f32[80,256]{1,0:T(8,128)S(1)} all-gather(f32[40,256]{1,0:T(8,128)S(1)} %concatenate.10), channel_id=2, replica_groups=mesh['x'=4,'z'=8,'core'=2,'y'=8] {'core'}, dimensions={0}, use_global_device_ids=true | all-gather | bytes 122880 | tf_op jit(solution)/shard_map/all_gather | solution.py:132
  52.8 0.7 concatenate.11
  53.5 34.6 %all_to_all.30 = f32[32,24,256]{2,1,0:T(8,128)S(1)} all-to-all(f32[32,24,256]{2,1,0:T(8,128)S(1)} %broadcast_in_dim.33), channel_id=1, replica_groups=mesh['x'=4,'z'=8,'core'=2,'y'=8] {'x','z'}, dimensions={0} | all-to-all | bytes 1572864 | tf_op jit(solution)/shard_map/all_to_all | solution.py:95
  88.2 6.2 %all_gather.29 = f32[32,256]{1,0:T(8,128)S(1)} all-gather(f32[16,256]{1,0:T(8,128)S(1)} %multiply_add_fusion.4), channel_id=1, replica_groups=mesh['x'=4,'z'=8,'core'=2,'y'=8] {'core'}, dimensions={0}, use_global_device_ids=true | all-gather | bytes 49152 | tf_op jit(solution)/shard_map/all_gather | solution.py:142
  94.5 8.1 %shard_map.79 = f32[16,256]{1,0:T(8,128)S(1)} custom-call(s32[1]{0:T(128)} %bitcast.14.live_ref, s32[96]{0:T(128)S(1)} %reshape.60.pairs_ref, f32[32,256]{1,0:T(8,128)S(1)} %negate_select_fusion.1.bias_ref, bf16[8192,128]{1,0:T(8,128)(2,1)S(1)} %pad.11.red_ref.col_ref, bf16[4096,128]{1,0:T(8,128)(2,1)S(1)} %pad.12.col_ref.red_ref), custom_call_target="tpu_custom_call" | custom-call | tf_op jit(solution)/shard_map/pallas_call | solution.py:78
  102.7 0.7 broadcast_in_dim.34
  103.3 8.7 %all-to-all-start.2 = ((f32[8,16,256]{2,1,0:T(8,128)}), f32[8,16,256]{2,1,0:T(8,128)S(1)}, u32[]{:S(2)}, u32[]{:S(2)}) async-start(f32[8,16,256]{2,1,0:T(8,128)} %broadcast_in_dim.34), calls=%async_computation.2 | async-start | bytes 262144 | tf_op jit(solution)/shard_map/all_to_all | solution.py:95
  112.0 7.8 %all-to-all-done.2 = f32[8,16,256]{2,1,0:T(8,128)S(1)} async-done(((f32[8,16,256]{2,1,0:T(8,128)}), f32[8,16,256]{2,1,0:T(8,128)S(1)}, u32[]{:S(2)}, u32[]{:S(2)}) %all-to-all-start.2) | async-done | bytes 131104 | tf_op jit(solution)/shard_map/all_to_all | solution.py:95
  119.9 8.2 %shard_map.80 = f32[32,256]{1,0:T(8,128)S(1)} custom-call(s32[1]{0:T(128)} %bitcast.15.live_ref, s32[96]{0:T(128)S(1)} %reshape.60.pairs_ref, f32[16,256]{1,0:T(8,128)S(1)} %negate_select_fusion.2.bias_ref, bf16[4096,128]{1,0:T(8,128)(2,1)S(1)} %pad.12.col_ref.red_ref, bf16[8192,128]{1,0:T(8,128)(2,1)S(1)} %pad.11.red_ref.col_ref), custom_call_target="tpu_custom_call" | custom-call | tf_op jit(solution)/shard_map/pallas_call | solution.py:78
  128.2 4.4 %all-gather.1 = f32[64,256]{1,0:T(8,128)S(1)} all-gather(f32[32,256]{1,0:T(8,128)S(1)} %shard_map.80), channel_id=3, replica_groups=mesh['x'=4,'z'=8,'core'=2,'y'=8] {'core'}, dimensions={0}, use_global_device_ids=true | all-gather | bytes 98304 | tf_op jit(solution)/shard_map/all_gather | solution.py:139
  132.6 27.3 %all_to_all.31 = f32[32,16,256]{2,1,0:T(8,128)} all-to-all(f32[32,16,256]{2,1,0:T(8,128)S(1)} %broadcast_in_dim.35), channel_id=1, replica_groups=mesh['x'=4,'z'=8,'core'=2,'y'=8] {'x','z'}, dimensions={0} | all-to-all | bytes 1048576 | tf_op jit(solution)/shard_map/all_to_all | solution.py:95
  160.0 1.1 reduce_max.86
  161.1 1.1 exponential_reduce_fusion.1
  162.2 5.1 %all_gather.32 = f32[32,256]{1,0:T(8,128)S(1)} all-gather(f32[16,256]{1,0:T(8,128)S(1)} %multiply_add_fusion.2), channel_id=1, replica_groups=mesh['x'=4,'z'=8,'core'=2,'y'=8] {'core'}, dimensions={0}, use_global_device_ids=true | all-gather | bytes 49152 | tf_op jit(solution)/shard_map/all_gather | solution.py:142
  167.4 8.1 %shard_map.81 = f32[16,256]{1,0:T(8,128)S(1)} custom-call(s32[1]{0:T(128)} %bitcast.16.live_ref, s32[96]{0:T(128)S(1)} %reshape.60.pairs_ref, f32[32,256]{1,0:T(8,128)S(1)} %negate_select_fusion.bias_ref, bf16[8192,128]{1,0:T(8,128)(2,1)S(1)} %pad.11.red_ref.col_ref, bf16[4096,128]{1,0:T(8,128)(2,1)S(1)} %pad.12.col_ref.red_ref), custom_call_target="tpu_custom_call" | custom-call | tf_op jit(solution)/shard_map/pallas_call | solution.py:78
  175.5 13.9 %all_to_all.32 = f32[8,16,256]{2,1,0:T(8,128)S(1)} all-to-all(f32[8,16,256]{2,1,0:T(8,128)S(1)} %broadcast_in_dim.36), channel_id=1, replica_groups=mesh['x'=4,'z'=8,'core'=2,'y'=8] {'y'}, dimensions={0} | all-to-all | bytes 262144 | tf_op jit(solution)/shard_map/all_to_all | solution.py:95
  189.6 8.2 %shard_map.82 = f32[32,256]{1,0:T(8,128)S(1)} custom-call(s32[1]{0:T(128)} %bitcast.17.live_ref, s32[96]{0:T(128)S(1)} %reshape.60.pairs_ref, f32[16,256]{1,0:T(8,128)S(1)} %get-tuple-element.2.bias_ref, bf16[4096,128]{1,0:T(8,128)(2,1)S(1)} %pad.12.col_ref.red_ref, bf16[8192,128]{1,0:T(8,128)(2,1)S(1)} %pad.11.red_ref.col_ref), custom_call_target="tpu_custom_call" | custom-call | tf_op jit(solution)/shard_map/pallas_call | solution.py:78
  197.8 3.7 %all-gather.2 = f32[64,256]{1,0:T(8,128)S(1)} all-gather(f32[32,256]{1,0:T(8,128)S(1)} %shard_map.82), channel_id=4, replica_groups=mesh['x'=4,'z'=8,'core'=2,'y'=8] {'core'}, dimensions={0}, use_global_device_ids=true | all-gather | bytes 98304 | tf_op jit(solution)/shard_map/all_gather | solution.py:139
  201.5 0.9 broadcast_in_dim.38
  202.4 13.5 %all-to-all-start.5 = ((f32[32,16,256]{2,1,0:T(8,128)}), f32[32,16,256]{2,1,0:T(8,128)S(1)}, u32[]{:S(2)}, u32[]{:S(2)}) async-start(f32[32,16,256]{2,1,0:T(8,128)} %broadcast_in_dim.38), calls=%async_computation.5 | async-start | bytes 1048576 | tf_op jit(solution)/shard_map/all_to_all | solution.py:95
  217.5 1.5 slice_reduce_fusion.2
  220.3 9.7 %all-to-all-done.5 = f32[32,16,256]{2,1,0:T(8,128)S(1)} async-done(((f32[32,16,256]{2,1,0:T(8,128)}), f32[32,16,256]{2,1,0:T(8,128)S(1)}, u32[]{:S(2)}, u32[]{:S(2)}) %all-to-all-start.5) | async-done | bytes 524320 | tf_op jit(solution)/shard_map/all_to_all | solution.py:95
  230.2 5.1 %all_gather.35 = f32[32,256]{1,0:T(8,128)S(1)} all-gather(f32[16,256]{1,0:T(8,128)S(1)} %multiply_add_fusion), channel_id=1, replica_groups=mesh['x'=4,'z'=8,'core'=2,'y'=8] {'core'}, dimensions={0}, use_global_device_ids=true | all-gather | bytes 49152 | tf_op jit(solution)/shard_map/all_gather | solution.py:142
  235.3 0.6 copy.32
  (66 shorter events, 5.7 us)
Async XLA Ops:
  0.6 2.9 %copy-start.1 = (bf16[8192,64]{0,1:T(8,128)(2,1)S(1)}, bf16[8192,64]{0,1:T(8,128)(2,1)}, u32[]{:S(2)}) copy-start(bf16[8192,64]{0,1:T(8,128)(2,1)} %param.7) | copy-start | bytes 3145732
  0.6 3.2 %copy-start.3 = (bf16[4096,64]{0,1:T(8,128)(2,1)S(1)}, bf16[4096,64]{0,1:T(8,128)(2,1)}, u32[]{:S(2)}) copy-start(bf16[4096,64]{0,1:T(8,128)(2,1)} %param.6) | copy-start | bytes 1572868
  5.2 2.1 copy-start.2
  7.3 0.7 copy-start.7
  7.3 1.6 copy-start.5
  7.9 20.9 %copy-start.6 = (s32[16]{0:T(128)S(1)}, s32[16]{0:T(128)}, u32[]{:S(2)}) copy-start(s32[16]{0:T(128)} %param.8) | copy-start | bytes 196
  19.0 18.5 %all-to-all-start = ((f32[8,24,256]{2,1,0:T(8,128)}), f32[8,24,256]{2,1,0:T(8,128)S(1)}, u32[]{:S(2)}, u32[]{:S(2)}) async-start(f32[8,24,256]{2,1,0:T(8,128)} %broadcast_in_dim.31), calls=%async_computation | async-start | bytes 393216 | tf_op jit(solution)/shard_map/all_to_all | solution.py:95
  88.1 6.5 %copy-start = (f32[32,24,256]{2,1,0:T(8,128)}, f32[32,24,256]{2,1,0:T(8,128)S(1)}, u32[]{:S(2)}) copy-start(f32[32,24,256]{2,1,0:T(8,128)S(1)} %all_to_all.30) | copy-start | bytes 2359300
  103.3 16.5 %all-to-all-start.2 = ((f32[8,16,256]{2,1,0:T(8,128)}), f32[8,16,256]{2,1,0:T(8,128)S(1)}, u32[]{:S(2)}, u32[]{:S(2)}) async-start(f32[8,16,256]{2,1,0:T(8,128)} %broadcast_in_dim.34), calls=%async_computation.2 | async-start | bytes 262144 | tf_op jit(solution)/shard_map/all_to_all | solution.py:95
  197.8 18.2 %copy-start.4 = (bf16[4096,64]{0,1:T(8,128)(2,1)S(1)}, bf16[4096,64]{0,1:T(8,128)(2,1)}, u32[]{:S(2)}) copy-start(bf16[4096,64]{0,1:T(8,128)(2,1)} %param.6) | copy-start | bytes 1572868
  202.4 27.6 %all-to-all-start.5 = ((f32[32,16,256]{2,1,0:T(8,128)}), f32[32,16,256]{2,1,0:T(8,128)S(1)}, u32[]{:S(2)}, u32[]{:S(2)}) async-start(f32[32,16,256]{2,1,0:T(8,128)} %broadcast_in_dim.38), calls=%async_computation.5 | async-start | bytes 1048576 | tf_op jit(solution)/shard_map/all_to_all | solution.py:95

commit v2 on v1

v2 whole, which is shorter than its diff:
```python
import functools
import math

import jax
import jax.numpy as jnp
from jax import lax
from jax.experimental import pallas as pl
from jax.experimental.pallas import tpu as pltpu
from jax.sharding import Mesh, PartitionSpec as P

BLOCK = 256
ITERS = 3
LANES = 128
GROUP = 8

epsilon = 0.05
very_low = -1e30
DIM = 64
SCALE = 2.0 / (DIM * epsilon) * math.log2(math.e)
INV_SCALE = 1.0 / SCALE

SMEM = pl.BlockSpec(memory_space=pltpu.SMEM)
VMEM = pl.BlockSpec(memory_space=pltpu.VMEM)
PARAMS = pltpu.CompilerParams(vmem_limit_bytes=24 * 1024 * 1024)


def total_count(counts_ref):
    return lax.fori_loop(0, counts_ref.shape[0], lambda i, s: s + counts_ref[i], 0).astype(jnp.float32)


def merged(parts):
    top = jnp.max(parts, axis=0)
    total = jnp.sum(jnp.exp2((parts - top[None]) * SCALE), axis=0)
    return top + jnp.log2(total) * INV_SCALE


def prepare_kernel(counts_s, counts_t, src_t, tgt_t, src, tgt, half_s, half_t, real_s, real_t):
    lane = lax.broadcasted_iota(jnp.int32, (1, LANES), 1)
    for counts, points, out, norms, real in (
        (counts_s, src_t, src, half_s, real_s),
        (counts_t, tgt_t, tgt, half_t, real_t),
    ):
        for row in range(norms.shape[0]):
            chunk = points[:, row * LANES : (row + 1) * LANES].astype(jnp.float32)
            norms[row : row + 1, :] = 0.5 * jnp.sum(chunk * chunk, axis=0, keepdims=True)
            chunk = jnp.concatenate([chunk, jnp.zeros((LANES - DIM, LANES), jnp.float32)], axis=0)
            out[row * LANES : (row + 1) * LANES, :] = chunk.T.astype(jnp.bfloat16)
            slot = lane + (row % 2) * LANES
            real[row : row + 1, :] = (slot < counts[row // 2]).astype(jnp.float32)


def prepare(src_counts, tgt_counts, src_t, tgt_t):
    ns, nt = src_t.shape[1], tgt_t.shape[1]
    rows_s = jax.ShapeDtypeStruct((ns // LANES, LANES), jnp.float32)
    rows_t = jax.ShapeDtypeStruct((nt // LANES, LANES), jnp.float32)
    return pl.pallas_call(
        prepare_kernel,
        out_shape=(
            jax.ShapeDtypeStruct((ns, LANES), jnp.bfloat16),
            jax.ShapeDtypeStruct((nt, LANES), jnp.bfloat16),
            rows_s,
            rows_t,
            rows_s,
            rows_t,
        ),
        in_specs=[SMEM, SMEM, VMEM, VMEM],
        out_specs=(VMEM,) * 6,
        compiler_params=PARAMS,
    )(src_counts, tgt_counts, src_t, tgt_t)


def sweep_kernel(
    side, live_ref, pairs_ref, counts_ref, parts_ref, real_ref, red_ref, col_ref,
    out_ref, rows_in, rows_out, peak, mass, ta, tb,
):
    nred = red_ref.shape[0] // BLOCK
    ncol = col_ref.shape[0] // BLOCK
    if len(parts_ref.shape) == 3:
        value = merged(parts_ref[:, : 2 * nred, :])
    else:
        gap = parts_ref.shape[0] // (2 * nred)
        value = parts_ref[pl.ds(0, 2 * nred, stride=gap), :] if gap > 1 else parts_ref[...]
    rows_in[...] = jnp.where(real_ref[...] > 0.0, -value, very_low)
    bias = jnp.concatenate([rows_in[pl.ds(h, nred, stride=2), :] for h in (0, 1)], axis=1)
    hi = bias.astype(jnp.bfloat16).astype(jnp.float32)
    rest = bias - hi
    mid = rest.astype(jnp.bfloat16).astype(jnp.float32)
    low = rest - mid
    blank = jnp.zeros((DIM, BLOCK), jnp.float32)
    half = DIM // 2
    if nred < half:
        pad = jnp.zeros((half - nred, BLOCK), jnp.float32)
        hi, mid, low = (jnp.concatenate([v, pad], axis=0) for v in (hi, mid, low))
    ta[...] = jnp.concatenate([blank, hi, mid], axis=0).T.astype(jnp.bfloat16)
    tb[...] = jnp.concatenate([low, blank, blank[:half]], axis=0).T.astype(jnp.bfloat16)
    peak[...] = jnp.full(peak.shape, very_low, jnp.float32)
    mass[...] = jnp.zeros(mass.shape, jnp.float32)
    lane = lax.broadcasted_iota(jnp.int32, (1, LANES), 1)
    live = live_ref[0, 0]

    def tile(t):
        red = pairs_ref[side, t]
        col = pairs_ref[1 - side, t]
        slot = jnp.where(t < live, col, ncol)
        one_a = ((lane == DIM + red) | (lane == DIM + half + red)).astype(jnp.float32).astype(jnp.bfloat16)
        one_b = (lane == red).astype(jnp.float32).astype(jnp.bfloat16)
        lhs = red_ref[pl.ds(pl.multiple_of(red * BLOCK, BLOCK), BLOCK), :] + ta[...]
        rhs = col_ref[pl.ds(pl.multiple_of(col * BLOCK, BLOCK), BLOCK), :] + one_a
        lhs = jnp.concatenate([lhs, tb[...]], axis=1)
        rhs = jnp.concatenate([rhs, jnp.broadcast_to(one_b, (BLOCK, LANES))], axis=1)
        score = lax.dot_general(
            lhs, rhs, (((1,), (1,)), ((), ())), preferred_element_type=jnp.float32
        ).reshape(BLOCK // 8, 8, BLOCK)
        old = peak[slot]
        new = jnp.maximum(old, jnp.max(score, axis=0))
        total = jnp.sum(jnp.exp2((score - new[None]) * SCALE), axis=0)
        mass[slot] = mass[slot] * jnp.exp2((old - new) * SCALE) + total
        peak[slot] = new

    def group(i, _):
        for u in range(GROUP):
            tile(i * GROUP + u)
        return 0

    lax.fori_loop(0, (live + GROUP - 1) // GROUP, group, 0)
    tops = peak[:ncol]
    top = jnp.max(tops, axis=1, keepdims=True)
    total = jnp.sum(mass[:ncol] * jnp.exp2((tops - top) * SCALE), axis=1)
    top = top.reshape(ncol, BLOCK)
    used = total > 0.0
    part = jnp.where(used, top + jnp.log2(jnp.where(used, total, 1.0)) * INV_SCALE, very_low)
    for h in (0, 1):
        rows_out[pl.ds(h, ncol, stride=2), :] = part[:, h * LANES : (h + 1) * LANES]
    if len(out_ref.shape) == 2:
        out_ref[...] = rows_out[...]
    else:
        out_ref[:, : 2 * ncol, :] = jnp.broadcast_to(rows_out[...][None], (out_ref.shape[0], 2 * ncol, LANES))
        extra = out_ref.shape[1] - 2 * ncol
        if extra:
            out_ref[:, 2 * ncol :, :] = jnp.full((out_ref.shape[0], extra, LANES), total_count(counts_ref))


def sweep(side, out, live, pairs, counts, parts, real, red, col):
    nred, ncol = red.shape[0] // BLOCK, col.shape[0] // BLOCK
    return pl.pallas_call(
        functools.partial(sweep_kernel, side),
        out_shape=jax.ShapeDtypeStruct(out, jnp.float32),
        in_specs=[SMEM, SMEM, SMEM, VMEM, VMEM, VMEM, VMEM],
        out_specs=VMEM,
        scratch_shapes=[
            pltpu.VMEM((2 * nred, LANES), jnp.float32),
            pltpu.VMEM((2 * ncol, LANES), jnp.float32),
            pltpu.VMEM((ncol + 1, 8, BLOCK), jnp.float32),
            pltpu.VMEM((ncol + 1, 8, BLOCK), jnp.float32),
            pltpu.VMEM((BLOCK, LANES), jnp.bfloat16),
            pltpu.VMEM((BLOCK, LANES), jnp.bfloat16),
        ],
        compiler_params=PARAMS,
    )(live, pairs, counts, parts, real, red, col)


def shard_kernel(counts_ref, parts_ref, out_ref):
    count = parts_ref.shape[0]
    value = jnp.broadcast_to(merged(parts_ref[...])[None], (count, LANES))
    if out_ref.shape[0] == count:
        out_ref[...] = value
    else:
        out_ref[pl.ds(0, count, stride=2), :] = value
        out_ref[pl.ds(1, count, stride=2), :] = jnp.full((count, LANES), total_count(counts_ref))


def shard(counts, parts, rows):
    return pl.pallas_call(
        shard_kernel,
        out_shape=jax.ShapeDtypeStruct((rows, LANES), jnp.float32),
        in_specs=[SMEM, VMEM],
        out_specs=VMEM,
        compiler_params=PARAMS,
    )(counts, parts)


def on_device(rows, cols, src_points, tgt_points, src_counts, tgt_counts, tile_list, tile_count):
    pairs = tile_list.reshape(tile_list.shape[2:]).T
    src, tgt, src_half, tgt_half, src_real, tgt_real = prepare(
        src_counts, tgt_counts, src_points.T, tgt_points.T
    )
    src_rows = src_half.shape[0]
    tgt_rows = tgt_half.shape[0]
    row = ("x", "z", "core")

    tgt_part = tgt_half
    for step in range(ITERS):
        extra = 8 if step == 0 else 0
        src_parts = sweep(
            1, (cols, src_rows + extra, LANES), tile_count, pairs, tgt_counts, tgt_part, tgt_real, tgt, src
        )
        src_parts = lax.all_to_all(src_parts, "y", 0, 0)
        part = sweep(0, (tgt_rows, LANES), tile_count, pairs, src_counts, src_parts, src_real, src, tgt)
        part = lax.all_to_all(part, row, 0, 0, tiled=True)
        part = shard(src_counts, part, 2 * rows if step == 0 else rows)
        tgt_part = lax.all_to_all(part, row, 0, 0, tiled=True)
        if step == 0:
            tgt_total = jnp.sum(src_parts[:, src_rows, 0])
            src_total = jnp.sum(tgt_part.reshape(rows, 2, LANES)[:, 1, 0])
    log_src = jnp.log(src_total)
    log_tgt = jnp.log(tgt_total)
    src_shift = -epsilon * (ITERS * log_src - (ITERS - 1) * log_tgt)
    tgt_shift = epsilon * ITERS * (log_src - log_tgt)
    src_out = jnp.where(src_real > 0.0, (src_half - merged(src_parts)) * (2.0 / DIM) + src_shift, 0.0)
    tgt_out = jnp.where(tgt_real > 0.0, (tgt_half - tgt_part) * (2.0 / DIM) + tgt_shift, 0.0)
    return (src_out.reshape(-1), tgt_out.reshape(-1))


def solution(mesh):
    rows, cols = mesh.shape["row"], mesh.shape["col"]
    fine = Mesh(mesh.devices.reshape(4, 8, 2, cols), ("x", "z", "core", "y"))
    row = ("x", "z", "core")
    return jax.shard_map(
        functools.partial(on_device, rows, cols),
        mesh=fine,
        in_specs=(P(row, None), P("y", None), P(row), P("y"), P(row, "y", None, None), P(row, "y")),
        out_specs=(P(row), P("y")),
        check_vma=False,
    )
```

time: 237 us -> 177 us (0.75)
  Pallas kernels: 49 us -> 27.6 us
  starting transfers between devices: 32.1 us -> 14.5 us
  blocking collectives: 106 us -> 97.9 us
  other arithmetic: 8.42 us -> 2.62 us
  local copies, waits for them, and re-layouts: 10.9 us -> 6.25 us
    all_gather x6 -> x0, blocking collectives: 30.6 us -> none  [the longest x3 16.4 us: on_device(): tgt_pot = -lax.all_gather(merged(parts), 'core', axis=0, tiled=True)]
    pallas_call x6, Pallas kernels: 49 us -> 23.7 us  [sweep(): pl.pallas_call(functools.partial(sweep_kernel, side), out_shape=jax.Shape...]
    all_to_all x3 -> x6, blocking collectives: 75.8 us -> 97.9 us  [the longest x2 41.5 us: on_device(): part = lax.all_to_all(part, row, 0, 0, tiled=True)]
    all_to_all x3, starting transfers between devices: 32.1 us -> 14.5 us  [the longest x1 6.47 us: on_device(): part = lax.all_to_all(part, row, 0, 0, tiled=True)]
    pallas_call x0 -> x4, Pallas kernels: none -> 3.88 us  [the longest x3 2.42 us: shard(): pl.pallas_call(shard_kernel, out_shape=jax.ShapeDtypeStruct((rows, LANES)...]
    reduce_sum x7 -> x2, other arithmetic: 4.41 us -> 1.32 us  [the longest x1 0.69 us: on_device(): src_total = jnp.sum(tgt_part.reshape(rows, 2, LANES)[:, 1, 0])]
    unnamed x21 -> x26, local copies, waits for them, and re-layouts: 5.44 us -> 6.25 us
  transfers between devices with their start and end apart: 3 -> 3, of which waited for: 3 -> 3; matrix products, arithmetic and copies ran while one was open for 2% -> 1% of each run, Pallas kernels for 0% -> 0%
where the time goes in v2:
time: 177 us; the launch traced here: 176 us
  blocking collectives  97.9 us (55%)
  Pallas kernels  27.6 us (16%)
  waiting for transfers between devices  24.7 us (14%)
  starting transfers between devices  14.5 us (8%)
  local copies, waits for them, and re-layouts  6.25 us (4%)
  between operations  2.83 us (2%)
  other arithmetic  2.62 us (1%)
    all_to_all x2, blocking collectives, on_device(): part = lax.all_to_all(part, row, 0, 0, tiled=True)  41.5 us
    all_to_all x2, blocking collectives, on_device(): src_parts = lax.all_to_all(src_parts, 'y', 0, 0)  29.4 us
    all_to_all x2, blocking collectives, on_device(): tgt_part = lax.all_to_all(part, row, 0, 0, tiled=True)  27.1 us
    pallas_call x6, Pallas kernels, sweep(): pl.pallas_call(functools.partial(sweep_kernel, side), out_shape=jax.Shape...  23.7 us
    all_to_all x1, waiting for transfers between devices, on_device(): part = lax.all_to_all(part, row, 0, 0, tiled=True)  9.22 us
    all_to_all x1, waiting for transfers between devices, on_device(): tgt_part = lax.all_to_all(part, row, 0, 0, tiled=True)  8.76 us
    all_to_all x1, waiting for transfers between devices, on_device(): src_parts = lax.all_to_all(src_parts, 'y', 0, 0)  6.73 us
    all_to_all x1, starting transfers between devices, on_device(): part = lax.all_to_all(part, row, 0, 0, tiled=True)  6.47 us
  transfers between devices with their start and end apart: 3, of which 3 were waited for; matrix products, arithmetic and copies ran while one was open for 1% of the time, Pallas kernels for 0%

profile of v2, /device:TPU:1, one launch (start us, length us, event | category | flops | bytes accessed | tf_op | source)
XLA Modules:
  0.0 176.4 jit_solution(9423916724196876076)
XLA Ops:
  1.3 1.2 copy-done
  2.5 1.0 copy-done.2
  3.5 0.7 copy-done.7
  4.2 0.7 copy-done.11
  4.9 1.5 shard_map.77
  6.4 0.7 copy-done.5
  7.0 3.9 %shard_map.78 = f32[8,40,128]{2,1,0:T(8,128)S(1)} custom-call(s32[1,1]{1,0:T(1,128)S(6)} %copy.13.live_ref, s32[2,48]{1,0:T(2,128)S(1)} %bitcast.42, s32[32]{0:T(128)S(1)} %copy-done.11, f32[64,128]{1,0:T(8,128)S(1)} %get-tuple-element.10.parts_ref, f32[64,128]{1,0:T(8,128)S(1)} %get-tuple-element.11.real_ref, ...), custom_call_target="tpu_custom_call" | custom-call | tf_op jit(solution)/shard_map/pallas_call | solution.py:145
  11.0 17.4 %all_to_all.82.parts_ref = f32[8,40,128]{2,1,0:T(8,128)S(1)} all-to-all(f32[8,40,128]{2,1,0:T(8,128)S(1)} %shard_map.78), channel_id=1, replica_groups=mesh['x'=4,'z'=8,'core'=2,'y'=8] {'y'}, dimensions={0} | all-to-all | bytes 327680 | tf_op jit(solution)/shard_map/all_to_all | solution.py:197
  28.4 3.9 %shard_map.79 = f32[64,128]{1,0:T(8,128)S(1)} custom-call(s32[1,1]{1,0:T(1,128)S(6)} %copy.13.live_ref, s32[2,48]{1,0:T(2,128)S(1)} %bitcast.43, s32[16]{0:T(128)S(1)} %copy-done.7, f32[8,40,128]{2,1,0:T(8,128)S(1)} %all_to_all.82.parts_ref, f32[32,128]{1,0:T(8,128)S(1)} %get-tuple-element.8.real_ref, ...), custom_call_target="tpu_custom_call" | custom-call | tf_op jit(solution)/shard_map/pallas_call | solution.py:145
  32.3 26.2 %all_to_all.83 = f32[64,1,128]{2,1,0:T(1,128)S(1)} all-to-all(f32[64,1,128]{2,1,0:T(1,128)S(1)} %bitcast.37), channel_id=1, replica_groups=mesh['x'=4,'z'=8,'core'=2,'y'=8] {'x','z','core'}, dimensions={0} | all-to-all | bytes 65536 | tf_op jit(solution)/shard_map/all_to_all | solution.py:199
  58.4 0.7 shard_map.80
  59.1 13.8 %all_to_all.84 = f32[64,2,128]{2,1,0:T(2,128)S(1)} all-to-all(f32[64,2,128]{2,1,0:T(2,128)S(1)} %bitcast.34), channel_id=1, replica_groups=mesh['x'=4,'z'=8,'core'=2,'y'=8] {'x','z','core'}, dimensions={0} | all-to-all | bytes 131072 | tf_op jit(solution)/shard_map/all_to_all | solution.py:201
  72.9 3.7 %shard_map.81 = f32[8,32,128]{2,1,0:T(8,128)S(1)} custom-call(s32[1,1]{1,0:T(1,128)S(6)} %copy.13.live_ref, s32[2,48]{1,0:T(2,128)S(1)} %bitcast.44, s32[32]{0:T(128)S(1)} %copy-done.12, f32[128,128]{1,0:T(8,128)S(1)} %bitcast.33, f32[64,128]{1,0:T(8,128)S(1)} %get-tuple-element.11.real_ref, bf16[8192,128]{1,0:T(8,128)(2,1)S(1)} %get-tuple-element.12.red_ref.col_ref, ...), custom_call_target="tpu_custom_call" | custom-call | tf_op jit(solution)/shard_map/pallas_call | solution.py:145
  76.6 12.0 %all_to_all.85.parts_ref = f32[8,32,128]{2,1,0:T(8,128)S(1)} all-to-all(f32[8,32,128]{2,1,0:T(8,128)S(1)} %shard_map.81), channel_id=1, replica_groups=mesh['x'=4,'z'=8,'core'=2,'y'=8] {'y'}, dimensions={0} | all-to-all | bytes 262144 | tf_op jit(solution)/shard_map/all_to_all | solution.py:197
  88.6 3.9 %shard_map.82 = f32[64,128]{1,0:T(8,128)S(1)} custom-call(s32[1,1]{1,0:T(1,128)S(6)} %copy.13.live_ref, s32[2,48]{1,0:T(2,128)S(1)} %bitcast.45, s32[16]{0:T(128)S(1)} %copy-done.7, f32[8,32,128]{2,1,0:T(8,128)S(1)} %all_to_all.85.parts_ref, f32[32,128]{1,0:T(8,128)S(1)} %get-tuple-element.8.real_ref, ...), custom_call_target="tpu_custom_call" | custom-call | tf_op jit(solution)/shard_map/pallas_call | solution.py:145
  92.5 15.3 %all_to_all.86 = f32[64,1,128]{2,1,0:T(1,128)S(1)} all-to-all(f32[64,1,128]{2,1,0:T(1,128)S(1)} %bitcast.35), channel_id=1, replica_groups=mesh['x'=4,'z'=8,'core'=2,'y'=8] {'x','z','core'}, dimensions={0} | all-to-all | bytes 65536 | tf_op jit(solution)/shard_map/all_to_all | solution.py:199
  108.4 13.3 %all_to_all.87 = f32[64,1,128]{2,1,0:T(1,128)S(1)} all-to-all(f32[64,1,128]{2,1,0:T(1,128)S(1)} %bitcast.41), channel_id=1, replica_groups=mesh['x'=4,'z'=8,'core'=2,'y'=8] {'x','z','core'}, dimensions={0} | all-to-all | bytes 65536 | tf_op jit(solution)/shard_map/all_to_all | solution.py:201
  121.7 3.7 %shard_map.84 = f32[8,32,128]{2,1,0:T(8,128)S(1)} custom-call(s32[1,1]{1,0:T(1,128)S(6)} %copy.13.live_ref, s32[2,48]{1,0:T(2,128)S(1)} %bitcast.46, s32[32]{0:T(128)S(1)} %copy-done.12, f32[64,128]{1,0:T(8,128)S(1)} %bitcast.36, f32[64,128]{1,0:T(8,128)S(1)} %get-tuple-element.11.real_ref, bf16[8192,128]{1,0:T(8,128)(2,1)S(1)} %get-tuple-element.12.red_ref.col_ref, ...), custom_call_target="tpu_custom_call" | custom-call | tf_op jit(solution)/shard_map/pallas_call | solution.py:145
  125.5 0.6 copy-done.1
  126.1 3.4 %all-to-all-start.6 = ((f32[8,32,128]{2,1,0:T(8,128)}), f32[8,32,128]{2,1,0:T(8,128)S(1)}, u32[]{:S(2)}, u32[]{:S(2)}) async-start(f32[8,32,128]{2,1,0:T(8,128)} %copy-done.1), calls=%async_computation.6 | async-start | bytes 262144 | tf_op jit(solution)/shard_map/all_to_all | solution.py:197
  129.5 0.6 slice_reduce_fusion.1
  130.8 0.7 slice_reduce_fusion
  132.2 6.7 %all-to-all-done.6.parts_ref = f32[8,32,128]{2,1,0:T(8,128)S(1)} async-done(((f32[8,32,128]{2,1,0:T(8,128)}), f32[8,32,128]{2,1,0:T(8,128)S(1)}, u32[]{:S(2)}, u32[]{:S(2)}) %all-to-all-start.6) | async-done | bytes 131104 | tf_op jit(solution)/shard_map/all_to_all | solution.py:197
  138.9 0.7 copy-done.6
  139.6 0.7 copy-done.8
  140.3 4.5 %shard_map.85 = f32[64,128]{1,0:T(8,128)} custom-call(s32[1,1]{1,0:T(1,128)S(6)} %copy.13.live_ref, s32[2,48]{1,0:T(2,128)S(1)} %bitcast.47, s32[16]{0:T(128)S(1)} %copy-done.8, f32[8,32,128]{2,1,0:T(8,128)S(1)} %all-to-all-done.6.parts_ref, f32[32,128]{1,0:T(8,128)S(1)} %get-tuple-element.8.real_ref, ...), custom_call_target="tpu_custom_call" | custom-call | tf_op jit(solution)/shard_map/pallas_call | solution.py:145
  144.8 6.5 %all-to-all-start.7 = ((f32[64,1,128]{2,1,0:T(1,128)}), f32[64,1,128]{2,1,0:T(1,128)S(1)}, u32[]{:S(2)}, u32[]{:S(2)}) async-start(f32[64,1,128]{2,1,0:T(1,128)} %bitcast.18), calls=%async_computation.7 | async-start | bytes 65536 | tf_op jit(solution)/shard_map/all_to_all | solution.py:199
  151.3 9.2 %all-to-all-done.7 = f32[64,1,128]{2,1,0:T(1,128)S(1)} async-done(((f32[64,1,128]{2,1,0:T(1,128)}), f32[64,1,128]{2,1,0:T(1,128)S(1)}, u32[]{:S(2)}, u32[]{:S(2)}) %all-to-all-start.7) | async-done | bytes 32800 | tf_op jit(solution)/shard_map/all_to_all | solution.py:199
  160.5 1.2 shard_map.86
  161.7 4.7 %all-to-all-start.8 = ((f32[64,1,128]{2,1,0:T(1,128)}), f32[64,1,128]{2,1,0:T(1,128)S(1)}, u32[]{:S(2)}, u32[]{:S(2)}) async-start(f32[64,1,128]{2,1,0:T(1,128)} %bitcast.21), calls=%async_computation.8 | async-start | bytes 65536 | tf_op jit(solution)/shard_map/all_to_all | solution.py:201
  166.4 0.6 select_bitcast_fusion.1
  167.0 8.8 %all-to-all-done.8 = f32[64,1,128]{2,1,0:T(1,128)S(1)} async-done(((f32[64,1,128]{2,1,0:T(1,128)}), f32[64,1,128]{2,1,0:T(1,128)S(1)}, u32[]{:S(2)}, u32[]{:S(2)}) %all-to-all-start.8) | async-done | bytes 32800 | tf_op jit(solution)/shard_map/all_to_all | solution.py:201
  (22 shorter events, 1.3 us)
Async XLA Ops:
  1.3 1.2 copy-start
  2.5 1.0 copy-start.2
  3.5 0.7 copy-start.7
  4.2 0.7 copy-start.11
  6.3 25.9 %copy-start.3 = (f32[64,128]{1,0:T(8,128)}, f32[64,128]{1,0:T(8,128)S(1)}, u32[]{:S(2)}) copy-start(f32[64,128]{1,0:T(8,128)S(1)} %get-tuple-element.10.parts_ref) | copy-start | bytes 98308
  6.3 25.9 %copy-start.9 = (f32[32,128]{1,0:T(8,128)}, f32[32,128]{1,0:T(8,128)S(1)}, u32[]{:S(2)}) copy-start(f32[32,128]{1,0:T(8,128)S(1)} %get-tuple-element.9) | copy-start | bytes 49156
  6.3 0.7 copy-start.5
  11.0 61.9 %copy-start.12 = (s32[32]{0:T(128)S(1)}, s32[32]{0:T(128)}, u32[]{:S(2)}) copy-start(s32[32]{0:T(128)} %counts_ref.15) | copy-start | bytes 388
  125.5 0.7 copy-start.1
  126.1 12.8 %all-to-all-start.6 = ((f32[8,32,128]{2,1,0:T(8,128)}), f32[8,32,128]{2,1,0:T(8,128)S(1)}, u32[]{:S(2)}, u32[]{:S(2)}) async-start(f32[8,32,128]{2,1,0:T(8,128)} %copy-done.1), calls=%async_computation.6 | async-start | bytes 262144 | tf_op jit(solution)/shard_map/all_to_all | solution.py:197
  130.1 45.7 %copy-start.4 = (f32[64,128]{1,0:T(8,128)S(1)}, f32[64,128]{1,0:T(8,128)}, u32[]{:S(2)}) copy-start(f32[64,128]{1,0:T(8,128)} %copy-done.3) | copy-start | bytes 98308
  138.9 0.7 copy-start.6
  139.6 0.7 copy-start.8
  140.3 26.1 %copy-start.10 = (f32[32,128]{1,0:T(8,128)S(1)}, f32[32,128]{1,0:T(8,128)}, u32[]{:S(2)}) copy-start(f32[32,128]{1,0:T(8,128)} %copy-done.9) | copy-start | bytes 49156
  144.8 15.8 %all-to-all-start.7 = ((f32[64,1,128]{2,1,0:T(1,128)}), f32[64,1,128]{2,1,0:T(1,128)S(1)}, u32[]{:S(2)}, u32[]{:S(2)}) async-start(f32[64,1,128]{2,1,0:T(1,128)} %bitcast.18), calls=%async_computation.7 | async-start | bytes 65536 | tf_op jit(solution)/shard_map/all_to_all | solution.py:199
  161.7 14.1 %all-to-all-start.8 = ((f32[64,1,128]{2,1,0:T(1,128)}), f32[64,1,128]{2,1,0:T(1,128)S(1)}, u32[]{:S(2)}, u32[]{:S(2)}) async-start(f32[64,1,128]{2,1,0:T(1,128)} %bitcast.21), calls=%async_computation.8 | async-start | bytes 65536 | tf_op jit(solution)/shard_map/all_to_all | solution.py:201

commit v3 on v2

--- a/solution.py
+++ b/solution.py
@@ -20,8 +20,13 @@
 INV_SCALE = 1.0 / SCALE
 
 SMEM = pl.BlockSpec(memory_space=pltpu.SMEM)
+HBM = pl.BlockSpec(memory_space=pltpu.HBM)
 VMEM = pl.BlockSpec(memory_space=pltpu.VMEM)
 PARAMS = pltpu.CompilerParams(vmem_limit_bytes=24 * 1024 * 1024)
+
+
+def in_hbm(*arrays):
+    return [pltpu.with_memory_space_constraint(a, pltpu.HBM) for a in arrays]
 
 
 def total_count(counts_ref):
@@ -34,12 +39,19 @@
     return top + jnp.log2(total) * INV_SCALE
 
 
-def prepare_kernel(counts_s, counts_t, src_t, tgt_t, src, tgt, half_s, half_t, real_s, real_t):
+def prepare_kernel(counts_s, counts_t, src_t, tgt_t, src, tgt, half_s, half_t, real_s, real_t, cs, ct, xs, xt, sems):
+    copies = [
+        pltpu.make_async_copy(a, b, sems.at[i])
+        for i, (a, b) in enumerate(((counts_s, cs), (src_t, xs), (counts_t, ct), (tgt_t, xt)))
+    ]
+    for copy in copies:
+        copy.start()
     lane = lax.broadcasted_iota(jnp.int32, (1, LANES), 1)
-    for counts, points, out, norms, real in (
-        (counts_s, src_t, src, half_s, real_s),
-        (counts_t, tgt_t, tgt, half_t, real_t),
+    for side, (counts, points, out, norms, real) in enumerate(
+        ((cs, xs, src, half_s, real_s), (ct, xt, tgt, half_t, real_t))
     ):
+        copies[2 * side].wait()
+        copies[2 * side + 1].wait()
         for row in range(norms.shape[0]):
             chunk = points[:, row * LANES : (row + 1) * LANES].astype(jnp.float32)
             norms[row : row + 1, :] = 0.5 * jnp.sum(chunk * chunk, axis=0, keepdims=True)
@@ -63,23 +75,35 @@
             rows_s,
             rows_t,
         ),
-        in_specs=[SMEM, SMEM, VMEM, VMEM],
+        in_specs=[HBM] * 4,
         out_specs=(VMEM,) * 6,
+        scratch_shapes=[
+            pltpu.SMEM(src_counts.shape, jnp.int32),
+            pltpu.SMEM(tgt_counts.shape, jnp.int32),
+            pltpu.VMEM(src_t.shape, jnp.bfloat16),
+            pltpu.VMEM(tgt_t.shape, jnp.bfloat16),
+            pltpu.SemaphoreType.DMA((4,)),
+        ],
         compiler_params=PARAMS,
-    )(src_counts, tgt_counts, src_t, tgt_t)
+    )(*in_hbm(src_counts, tgt_counts, src_t, tgt_t))
 
 
 def sweep_kernel(
-    side, live_ref, pairs_ref, counts_ref, parts_ref, real_ref, red_ref, col_ref,
-    out_ref, rows_in, rows_out, peak, mass, ta, tb,
+    side, live_ref, pairs_hbm, counts_hbm, parts_ref, real_ref, red_ref, col_ref,
+    out_ref, rows_in, rows_out, peak, mass, ta, tb, pairs_ref, counts_ref, sems,
 ):
+    fetches = [
+        pltpu.make_async_copy(a, b, sems.at[i])
+        for i, (a, b) in enumerate(((pairs_hbm, pairs_ref), (counts_hbm, counts_ref)))
+    ]
+    for fetch in fetches:
+        fetch.start()
     nred = red_ref.shape[0] // BLOCK
     ncol = col_ref.shape[0] // BLOCK
     if len(parts_ref.shape) == 3:
         value = merged(parts_ref[:, : 2 * nred, :])
     else:
-        gap = parts_ref.shape[0] // (2 * nred)
-        value = parts_ref[pl.ds(0, 2 * nred, stride=gap), :] if gap > 1 else parts_ref[...]
+        value = parts_ref[...]
     rows_in[...] = jnp.where(real_ref[...] > 0.0, -value, very_low)
     bias = jnp.concatenate([rows_in[pl.ds(h, nred, stride=2), :] for h in (0, 1)], axis=1)
     hi = bias.astype(jnp.bfloat16).astype(jnp.float32)
@@ -96,6 +120,8 @@
     peak[...] = jnp.full(peak.shape, very_low, jnp.float32)
     mass[...] = jnp.zeros(mass.shape, jnp.float32)
     lane = lax.broadcasted_iota(jnp.int32, (1, LANES), 1)
+    for fetch in fetches:
+        fetch.wait()
     live = live_ref[0, 0]
 
     def tile(t):
@@ -131,13 +157,10 @@
     part = jnp.where(used, top + jnp.log2(jnp.where(used, total, 1.0)) * INV_SCALE, very_low)
     for h in (0, 1):
         rows_out[pl.ds(h, ncol, stride=2), :] = part[:, h * LANES : (h + 1) * LANES]
-    if len(out_ref.shape) == 2:
-        out_ref[...] = rows_out[...]
-    else:
-        out_ref[:, : 2 * ncol, :] = jnp.broadcast_to(rows_out[...][None], (out_ref.shape[0], 2 * ncol, LANES))
-        extra = out_ref.shape[1] - 2 * ncol
-        if extra:
-            out_ref[:, 2 * ncol :, :] = jnp.full((out_ref.shape[0], extra, LANES), total_count(counts_ref))
+    copies, rows, _ = out_ref.shape
+    out_ref[:, : 2 * ncol, :] = jnp.broadcast_to(rows_out[...][None], (copies, 2 * ncol, LANES))
+    if rows > 2 * ncol:
+        out_ref[:, 2 * ncol :, :] = jnp.full((copies, rows - 2 * ncol, LANES), total_count(counts_ref))
 
 
 def sweep(side, out, live, pairs, counts, parts, real, red, col):
@@ -145,7 +168,7 @@
     return pl.pallas_call(
         functools.partial(sweep_kernel, side),
         out_shape=jax.ShapeDtypeStruct(out, jnp.float32),
-        in_specs=[SMEM, SMEM, SMEM, VMEM, VMEM, VMEM, VMEM],
+        in_specs=[SMEM, HBM, HBM, VMEM, VMEM, VMEM, VMEM],
         out_specs=VMEM,
         scratch_shapes=[
             pltpu.VMEM((2 * nred, LANES), jnp.float32),
@@ -154,69 +177,69 @@
             pltpu.VMEM((ncol + 1, 8, BLOCK), jnp.float32),
             pltpu.VMEM((BLOCK, LANES), jnp.bfloat16),
             pltpu.VMEM((BLOCK, LANES), jnp.bfloat16),
+            pltpu.SMEM(pairs.shape, jnp.int32),
+            pltpu.SMEM(counts.shape, jnp.int32),
+            pltpu.SemaphoreType.DMA((2,)),
         ],
         compiler_params=PARAMS,
-    )(live, pairs, counts, parts, real, red, col)
-
-
-def shard_kernel(counts_ref, parts_ref, out_ref):
-    count = parts_ref.shape[0]
-    value = jnp.broadcast_to(merged(parts_ref[...])[None], (count, LANES))
-    if out_ref.shape[0] == count:
-        out_ref[...] = value
-    else:
-        out_ref[pl.ds(0, count, stride=2), :] = value
-        out_ref[pl.ds(1, count, stride=2), :] = jnp.full((count, LANES), total_count(counts_ref))
-
-
-def shard(counts, parts, rows):
+    )(live, *in_hbm(pairs, counts), parts, real, red, col)
+
+
+def relay_kernel(rows, parts_ref, out_ref):
+    copies, height, _ = out_ref.shape
+    out_ref[:, :rows, :] = jnp.broadcast_to(merged(parts_ref[:, :rows, :])[None], (copies, rows, LANES))
+    if height > rows:
+        count = jnp.sum(parts_ref[:, rows:, :], axis=0)
+        out_ref[:, rows:, :] = jnp.broadcast_to(count[None], (copies, height - rows, LANES))
+
+
+def relay(rows, copies, parts):
     return pl.pallas_call(
-        shard_kernel,
-        out_shape=jax.ShapeDtypeStruct((rows, LANES), jnp.float32),
-        in_specs=[SMEM, VMEM],
+        functools.partial(relay_kernel, rows),
+        out_shape=jax.ShapeDtypeStruct((copies,) + parts.shape[1:], jnp.float32),
+        in_specs=[VMEM],
         out_specs=VMEM,
         compiler_params=PARAMS,
-    )(counts, parts)
-
-
-def on_device(rows, cols, src_points, tgt_points, src_counts, tgt_counts, tile_list, tile_count):
+    )(parts)
+
+
+def on_device(sizes, src_points, tgt_points, src_counts, tgt_counts, tile_list, tile_count):
     pairs = tile_list.reshape(tile_list.shape[2:]).T
     src, tgt, src_half, tgt_half, src_real, tgt_real = prepare(
         src_counts, tgt_counts, src_points.T, tgt_points.T
     )
     src_rows = src_half.shape[0]
     tgt_rows = tgt_half.shape[0]
-    row = ("x", "z", "core")
-
-    tgt_part = tgt_half
+
+    tgt_parts = tgt_half
     for step in range(ITERS):
         extra = 8 if step == 0 else 0
-        src_parts = sweep(
-            1, (cols, src_rows + extra, LANES), tile_count, pairs, tgt_counts, tgt_part, tgt_real, tgt, src
-        )
+        out = (sizes["y"], src_rows + extra, LANES)
+        src_parts = sweep(1, out, tile_count, pairs, tgt_counts, tgt_parts, tgt_real, tgt, src)
         src_parts = lax.all_to_all(src_parts, "y", 0, 0)
-        part = sweep(0, (tgt_rows, LANES), tile_count, pairs, src_counts, src_parts, src_real, src, tgt)
-        part = lax.all_to_all(part, row, 0, 0, tiled=True)
-        part = shard(src_counts, part, 2 * rows if step == 0 else rows)
-        tgt_part = lax.all_to_all(part, row, 0, 0, tiled=True)
+        out = (sizes["z"], tgt_rows + extra, LANES)
+        tgt_parts = sweep(0, out, tile_count, pairs, src_counts, src_parts, src_real, src, tgt)
+        tgt_parts = lax.all_to_all(tgt_parts, "z", 0, 0)
+        tgt_parts = relay(tgt_rows, sizes["x"] * sizes["core"], tgt_parts)
+        tgt_parts = lax.all_to_all(tgt_parts, ("x", "core"), 0, 0)
         if step == 0:
             tgt_total = jnp.sum(src_parts[:, src_rows, 0])
-            src_total = jnp.sum(tgt_part.reshape(rows, 2, LANES)[:, 1, 0])
+            src_total = jnp.sum(tgt_parts[:, tgt_rows, 0])
     log_src = jnp.log(src_total)
     log_tgt = jnp.log(tgt_total)
     src_shift = -epsilon * (ITERS * log_src - (ITERS - 1) * log_tgt)
     tgt_shift = epsilon * ITERS * (log_src - log_tgt)
     src_out = jnp.where(src_real > 0.0, (src_half - merged(src_parts)) * (2.0 / DIM) + src_shift, 0.0)
-    tgt_out = jnp.where(tgt_real > 0.0, (tgt_half - tgt_part) * (2.0 / DIM) + tgt_shift, 0.0)
+    tgt_out = jnp.where(tgt_real > 0.0, (tgt_half - merged(tgt_parts)) * (2.0 / DIM) + tgt_shift, 0.0)
     return (src_out.reshape(-1), tgt_out.reshape(-1))
 
 
 def solution(mesh):
-    rows, cols = mesh.shape["row"], mesh.shape["col"]
-    fine = Mesh(mesh.devices.reshape(4, 8, 2, cols), ("x", "z", "core", "y"))
+    sizes = {"x": 4, "z": 8, "core": 2, "y": mesh.shape["col"]}
+    fine = Mesh(mesh.devices.reshape(tuple(sizes.values())), tuple(sizes))
     row = ("x", "z", "core")
     return jax.shard_map(
-        functools.partial(on_device, rows, cols),
+        functools.partial(on_device, sizes),
         mesh=fine,
         in_specs=(P(row, None), P("y", None), P(row), P("y"), P(row, "y", None, None), P(row, "y")),
         out_specs=(P(row), P("y")),

time: 177 us -> 158 us (0.89)
  waiting for transfers between devices: 24.7 us -> 12.7 us
  local copies, waits for them, and re-layouts: 6.25 us -> 0 us
  blocking collectives: 97.9 us -> 104 us
  Pallas kernels: 27.6 us -> 22.8 us
    all_to_all x3 -> x2, waiting for transfers between devices: 24.7 us -> 12.7 us  [the longest x1 6.81 us: on_device(): tgt_parts = lax.all_to_all(tgt_parts, 'z', 0, 0)]
    all_to_all x2 -> x3, blocking collectives: 29.4 us -> 39.4 us  [on_device(): src_parts = lax.all_to_all(src_parts, 'y', 0, 0)]
    unnamed x26 -> x0, local copies, waits for them, and re-layouts: 6.25 us -> none
    all_to_all x4, blocking collectives: 68.6 us -> 64.2 us  [the longest x2 32.2 us: on_device(): tgt_parts = lax.all_to_all(tgt_parts, 'z', 0, 0)]
    pallas_call x6, Pallas kernels: 23.7 us -> 19.8 us  [sweep(): pl.pallas_call(functools.partial(sweep_kernel, side), out_shape=jax.Shape...]
    all_to_all x3 -> x2, starting transfers between devices: 14.5 us -> 12.9 us  [the longest x1 7.49 us: on_device(): tgt_parts = lax.all_to_all(tgt_parts, ('x', 'core'), 0, 0)]
  transfers between devices with their start and end apart: 3 -> 2, of which waited for: 3 -> 2; matrix products, arithmetic and copies ran while one was open for 1% -> 1% of each run, Pallas kernels for 0% -> 0%
where the time goes in v3:
time: 158 us; the launch traced here: 157 us
  blocking collectives  104 us (66%)
  Pallas kernels  22.8 us (14%)
  starting transfers between devices  12.9 us (8%)
  waiting for transfers between devices  12.7 us (8%)
  between operations  2.75 us (2%)
  other arithmetic  2.59 us (2%)
    all_to_all x3, blocking collectives, on_device(): src_parts = lax.all_to_all(src_parts, 'y', 0, 0)  39.4 us
    all_to_all x2, blocking collectives, on_device(): tgt_parts = lax.all_to_all(tgt_parts, 'z', 0, 0)  32.2 us
    all_to_all x2, blocking collectives, on_device(): tgt_parts = lax.all_to_all(tgt_parts, ('x', 'core'), 0, 0)  32 us
    pallas_call x6, Pallas kernels, sweep(): pl.pallas_call(functools.partial(sweep_kernel, side), out_shape=jax.Shape...  19.8 us
    all_to_all x1, starting transfers between devices, on_device(): tgt_parts = lax.all_to_all(tgt_parts, ('x', 'core'), 0, 0)  7.49 us
    all_to_all x1, waiting for transfers between devices, on_device(): tgt_parts = lax.all_to_all(tgt_parts, 'z', 0, 0)  6.81 us
    all_to_all x1, waiting for transfers between devices, on_device(): tgt_parts = lax.all_to_all(tgt_parts, ('x', 'core'), 0, 0)  5.84 us
    all_to_all x1, starting transfers between devices, on_device(): tgt_parts = lax.all_to_all(tgt_parts, 'z', 0, 0)  5.45 us
  transfers between devices with their start and end apart: 2, of which 2 were waited for; matrix products, arithmetic and copies ran while one was open for 1% of the time, Pallas kernels for 0%

profile of v3, /device:TPU:1, one launch (start us, length us, event | category | flops | bytes accessed | tf_op | source)
XLA Modules:
  0.0 157.3 jit_solution(13182911976326741072)
XLA Ops:
  1.3 2.1 %shard_map.77 = (bf16[4096,128]{1,0:T(8,128)(2,1)S(1)}, bf16[8192,128]{1,0:T(8,128)(2,1)S(1)}, f32[32,128]{1,0:T(8,128)S(1)}, f32[64,128]{1,0:T(8,128)S(1)}, f32...) custom-call(s32[16]{0:T(128)} %counts_hbm.11, s32[32]{0:T(128)} %counts_hbm.10, bf16[64,4096]{1,0:T(8,128)(2,1)} %bitcast.10, ...), custom_call_target="tpu_custom_call" | custom-call | tf_op jit(solution)/shard_map/pallas_call | solution.py:68
  3.4 3.2 %shard_map.78 = f32[8,40,128]{2,1,0:T(8,128)S(1)} custom-call(s32[1,1]{1,0:T(1,128)S(6)} %copy.8.live_ref, s32[2,48]{1,0:T(2,128)} %bitcast.11, s32[32]{0:T(128)} %counts_hbm.10, f32[64,128]{1,0:T(8,128)S(1)} %get-tuple-element.10.parts_ref, f32[64,128]{1,0:T(8,128)S(1)} %get-tuple-element.11.real_ref, ...), custom_call_target="tpu_custom_call" | custom-call | tf_op jit(solution)/shard_map/pallas_call | solution.py:168
  6.6 17.2 %all_to_all.45.parts_ref = f32[8,40,128]{2,1,0:T(8,128)S(1)} all-to-all(f32[8,40,128]{2,1,0:T(8,128)S(1)} %shard_map.78), channel_id=1, replica_groups=mesh['x'=4,'z'=8,'core'=2,'y'=8] {'y'}, dimensions={0} | all-to-all | bytes 327680 | tf_op jit(solution)/shard_map/all_to_all | solution.py:219
  23.9 3.3 %shard_map.79 = f32[8,72,128]{2,1,0:T(8,128)S(1)} custom-call(s32[1,1]{1,0:T(1,128)S(6)} %copy.8.live_ref, s32[2,48]{1,0:T(2,128)} %bitcast.12, s32[16]{0:T(128)} %counts_hbm.11, f32[8,40,128]{2,1,0:T(8,128)S(1)} %all_to_all.45.parts_ref, f32[32,128]{1,0:T(8,128)S(1)} %get-tuple-element.8.real_ref, bf16[4096,128]{1,0:T(8,128)(2,1)S(1)} %get-tuple-element.13.col_ref.red_ref, ...), custom_call_target="tpu_custom_call" | custom-call | tf_op jit(solution)/shard_map/pallas_call | solution.py:168
  27.2 18.8 %all_to_all.46.parts_ref = f32[8,72,128]{2,1,0:T(8,128)S(1)} all-to-all(f32[8,72,128]{2,1,0:T(8,128)S(1)} %shard_map.79), channel_id=1, replica_groups=mesh['x'=4,'z'=8,'core'=2,'y'=8] {'z'}, dimensions={0} | all-to-all | bytes 589824 | tf_op jit(solution)/shard_map/all_to_all | solution.py:222
  46.0 0.1 shard_map.80
  46.1 17.8 %all_to_all.47.parts_ref = f32[8,72,128]{2,1,0:T(8,128)S(1)} all-to-all(f32[8,72,128]{2,1,0:T(8,128)S(1)} %shard_map.80), channel_id=1, replica_groups=mesh['x'=4,'z'=8,'core'=2,'y'=8] {'x','core'}, dimensions={0} | all-to-all | bytes 589824 | tf_op jit(solution)/shard_map/all_to_all | solution.py:224
  63.9 3.1 %shard_map.81 = f32[8,32,128]{2,1,0:T(8,128)S(1)} custom-call(s32[1,1]{1,0:T(1,128)S(6)} %copy.8.live_ref, s32[2,48]{1,0:T(2,128)} %bitcast.13, s32[32]{0:T(128)} %counts_hbm.10, f32[8,72,128]{2,1,0:T(8,128)S(1)} %all_to_all.47.parts_ref, f32[64,128]{1,0:T(8,128)S(1)} %get-tuple-element.11.real_ref, bf16[8192,128]{1,0:T(8,128)(2,1)S(1)} %get-tuple-element.12.red_ref.col_ref, ...), custom_call_target="tpu_custom_call" | custom-call | tf_op jit(solution)/shard_map/pallas_call | solution.py:168
  67.0 11.3 %all_to_all.48.parts_ref = f32[8,32,128]{2,1,0:T(8,128)S(1)} all-to-all(f32[8,32,128]{2,1,0:T(8,128)S(1)} %shard_map.81), channel_id=1, replica_groups=mesh['x'=4,'z'=8,'core'=2,'y'=8] {'y'}, dimensions={0} | all-to-all | bytes 262144 | tf_op jit(solution)/shard_map/all_to_all | solution.py:219
  78.3 3.2 %shard_map.82 = f32[8,64,128]{2,1,0:T(8,128)S(1)} custom-call(s32[1,1]{1,0:T(1,128)S(6)} %copy.8.live_ref, s32[2,48]{1,0:T(2,128)} %bitcast.14, s32[16]{0:T(128)} %counts_hbm.11, f32[8,32,128]{2,1,0:T(8,128)S(1)} %all_to_all.48.parts_ref, f32[32,128]{1,0:T(8,128)S(1)} %get-tuple-element.8.real_ref, bf16[4096,128]{1,0:T(8,128)(2,1)S(1)} %get-tuple-element.13.col_ref.red_ref, ...), custom_call_target="tpu_custom_call" | custom-call | tf_op jit(solution)/shard_map/pallas_call | solution.py:168
  81.5 13.4 %all_to_all.49.parts_ref = f32[8,64,128]{2,1,0:T(8,128)S(1)} all-to-all(f32[8,64,128]{2,1,0:T(8,128)S(1)} %shard_map.82), channel_id=1, replica_groups=mesh['x'=4,'z'=8,'core'=2,'y'=8] {'z'}, dimensions={0} | all-to-all | bytes 524288 | tf_op jit(solution)/shard_map/all_to_all | solution.py:222
  94.9 0.1 shard_map.83
  95.0 14.1 %all_to_all.50.parts_ref = f32[8,64,128]{2,1,0:T(8,128)S(1)} all-to-all(f32[8,64,128]{2,1,0:T(8,128)S(1)} %shard_map.83), channel_id=1, replica_groups=mesh['x'=4,'z'=8,'core'=2,'y'=8] {'x','core'}, dimensions={0} | all-to-all | bytes 524288 | tf_op jit(solution)/shard_map/all_to_all | solution.py:224
  109.1 3.1 %shard_map.84 = f32[8,32,128]{2,1,0:T(8,128)S(1)} custom-call(s32[1,1]{1,0:T(1,128)S(6)} %copy.8.live_ref, s32[2,48]{1,0:T(2,128)} %bitcast.15, s32[32]{0:T(128)} %counts_hbm.10, f32[8,64,128]{2,1,0:T(8,128)S(1)} %all_to_all.50.parts_ref, f32[64,128]{1,0:T(8,128)S(1)} %get-tuple-element.11.real_ref, bf16[8192,128]{1,0:T(8,128)(2,1)S(1)} %get-tuple-element.12.red_ref.col_ref, ...), custom_call_target="tpu_custom_call" | custom-call | tf_op jit(solution)/shard_map/pallas_call | solution.py:168
  112.2 10.8 %all_to_all.51.parts_ref = f32[8,32,128]{2,1,0:T(8,128)S(1)} all-to-all(f32[8,32,128]{2,1,0:T(8,128)S(1)} %shard_map.84), channel_id=1, replica_groups=mesh['x'=4,'z'=8,'core'=2,'y'=8] {'y'}, dimensions={0} | all-to-all | bytes 262144 | tf_op jit(solution)/shard_map/all_to_all | solution.py:219
  123.1 3.9 %shard_map.85 = f32[8,64,128]{2,1,0:T(8,128)} custom-call(s32[1,1]{1,0:T(1,128)S(6)} %copy.8.live_ref, s32[2,48]{1,0:T(2,128)} %bitcast.16, s32[16]{0:T(128)} %counts_hbm.11, f32[8,32,128]{2,1,0:T(8,128)S(1)} %all_to_all.51.parts_ref, f32[32,128]{1,0:T(8,128)S(1)} %get-tuple-element.8.real_ref, bf16[4096,128]{1,0:T(8,128)(2,1)S(1)} %get-tuple-element.13.col_ref.red_ref, ...), custom_call_target="tpu_custom_call" | custom-call | tf_op jit(solution)/shard_map/pallas_call | solution.py:168
  127.0 5.5 %all-to-all-start.7 = ((f32[8,64,128]{2,1,0:T(8,128)}), f32[8,64,128]{2,1,0:T(8,128)S(1)}, u32[]{:S(2)}, u32[]{:S(2)}) async-start(f32[8,64,128]{2,1,0:T(8,128)} %shard_map.85), calls=%async_computation.7 | async-start | bytes 524288 | tf_op jit(solution)/shard_map/all_to_all | solution.py:222
  132.4 0.6 slice_reduce_fusion
  133.7 0.6 slice_reduce_fusion.1
  135.1 6.8 %all-to-all-done.7.parts_ref = f32[8,64,128]{2,1,0:T(8,128)S(1)} async-done(((f32[8,64,128]{2,1,0:T(8,128)}), f32[8,64,128]{2,1,0:T(8,128)S(1)}, u32[]{:S(2)}, u32[]{:S(2)}) %all-to-all-start.7) | async-done | bytes 262176 | tf_op jit(solution)/shard_map/all_to_all | solution.py:222
  141.9 0.8 shard_map.86
  142.6 7.5 %all-to-all-start.8 = ((f32[8,64,128]{2,1,0:T(8,128)}), f32[8,64,128]{2,1,0:T(8,128)S(1)}, u32[]{:S(2)}, u32[]{:S(2)}) async-start(f32[8,64,128]{2,1,0:T(8,128)} %shard_map.86), calls=%async_computation.8 | async-start | bytes 524288 | tf_op jit(solution)/shard_map/all_to_all | solution.py:224
  150.1 0.6 select_bitcast_fusion.1
  150.8 5.8 %all-to-all-done.8 = f32[8,64,128]{2,1,0:T(8,128)S(1)} async-done(((f32[8,64,128]{2,1,0:T(8,128)}), f32[8,64,128]{2,1,0:T(8,128)S(1)}, u32[]{:S(2)}, u32[]{:S(2)}) %all-to-all-start.8) | async-done | bytes 262176 | tf_op jit(solution)/shard_map/all_to_all | solution.py:224
  156.6 0.1 exponential_reduce_fusion
  156.7 0.6 select_bitcast_fusion
  (3 shorter events, 0.1 us)
Async XLA Ops:
  127.0 14.9 %all-to-all-start.7 = ((f32[8,64,128]{2,1,0:T(8,128)}), f32[8,64,128]{2,1,0:T(8,128)S(1)}, u32[]{:S(2)}, u32[]{:S(2)}) async-start(f32[8,64,128]{2,1,0:T(8,128)} %shard_map.85), calls=%async_computation.7 | async-start | bytes 524288 | tf_op jit(solution)/shard_map/all_to_all | solution.py:222
  142.6 14.0 %all-to-all-start.8 = ((f32[8,64,128]{2,1,0:T(8,128)}), f32[8,64,128]{2,1,0:T(8,128)S(1)}, u32[]{:S(2)}, u32[]{:S(2)}) async-start(f32[8,64,128]{2,1,0:T(8,128)} %shard_map.86), calls=%async_computation.8 | async-start | bytes 524288 | tf_op jit(solution)/shard_map/all_to_all | solution.py:224

commit v4 on v3

v4 whole, which is shorter than its diff:
```python
import functools
import math

import jax
import jax.numpy as jnp
from jax import lax
from jax.experimental import pallas as pl
from jax.experimental.pallas import tpu as pltpu
from jax.sharding import Mesh, PartitionSpec as P

BLOCK = 256
ITERS = 3
LANES = 128
GROUP = 16

epsilon = 0.05
very_low = -1e30
DIM = 64
SCALE = 2.0 / (DIM * epsilon) * math.log2(math.e)
INV_SCALE = 1.0 / SCALE

SMEM = pl.BlockSpec(memory_space=pltpu.SMEM)
HBM = pl.BlockSpec(memory_space=pltpu.HBM)
VMEM = pl.BlockSpec(memory_space=pltpu.VMEM)
PARAMS = pltpu.CompilerParams(vmem_limit_bytes=24 * 1024 * 1024)


def in_hbm(*arrays):
    return [pltpu.with_memory_space_constraint(a, pltpu.HBM) for a in arrays]


def merged(parts):
    top = jnp.max(parts, axis=0)
    total = jnp.sum(jnp.exp2((parts - top[None]) * SCALE), axis=0)
    return top + jnp.log2(total) * INV_SCALE


def prepare_kernel(counts_s, counts_t, src_t, tgt_t, src, tgt, half_s, half_t, real_s, real_t, sum_s, sum_t, cs, ct, xs, xt, sems):
    copies = [
        pltpu.make_async_copy(a, b, sems.at[i])
        for i, (a, b) in enumerate(((counts_s, cs), (src_t, xs), (counts_t, ct), (tgt_t, xt)))
    ]
    for copy in copies:
        copy.start()
    lane = lax.broadcasted_iota(jnp.int32, (1, LANES), 1)
    for side, (counts, points, out, norms, real, total) in enumerate(
        ((cs, xs, src, half_s, real_s, sum_s), (ct, xt, tgt, half_t, real_t, sum_t))
    ):
        copies[2 * side].wait()
        copies[2 * side + 1].wait()
        count = sum(counts[i] for i in range(counts.shape[0]))
        total[...] = jnp.full(total.shape, count).astype(jnp.float32)
        for row in range(norms.shape[0]):
            chunk = points[:, row * LANES : (row + 1) * LANES].astype(jnp.float32)
            norms[row : row + 1, :] = 0.5 * jnp.sum(chunk * chunk, axis=0, keepdims=True)
            chunk = jnp.concatenate([chunk, jnp.zeros((LANES - DIM, LANES), jnp.float32)], axis=0)
            out[row * LANES : (row + 1) * LANES, :] = chunk.T.astype(jnp.bfloat16)
            slot = lane + (row % 2) * LANES
            real[row : row + 1, :] = (slot < counts[row // 2]).astype(jnp.float32)


def prepare(src_counts, tgt_counts, src_t, tgt_t):
    ns, nt = src_t.shape[1], tgt_t.shape[1]
    rows_s = jax.ShapeDtypeStruct((ns // LANES, LANES), jnp.float32)
    rows_t = jax.ShapeDtypeStruct((nt // LANES, LANES), jnp.float32)
    total = jax.ShapeDtypeStruct((8, LANES), jnp.float32)
    return pl.pallas_call(
        prepare_kernel,
        out_shape=(
            jax.ShapeDtypeStruct((ns, LANES), jnp.bfloat16),
            jax.ShapeDtypeStruct((nt, LANES), jnp.bfloat16),
            rows_s,
            rows_t,
            rows_s,
            rows_t,
            total,
            total,
        ),
        in_specs=[HBM] * 4,
        out_specs=(VMEM,) * 8,
        scratch_shapes=[
            pltpu.SMEM(src_counts.shape, jnp.int32),
            pltpu.SMEM(tgt_counts.shape, jnp.int32),
            pltpu.VMEM(src_t.shape, jnp.bfloat16),
            pltpu.VMEM(tgt_t.shape, jnp.bfloat16),
            pltpu.SemaphoreType.DMA((4,)),
        ],
        compiler_params=PARAMS,
    )(*in_hbm(src_counts, tgt_counts, src_t, tgt_t))


def by_block(rows_ref):
    blocks = rows_ref.shape[0] // 2
    return jnp.concatenate([rows_ref[pl.ds(h, blocks, stride=2), :] for h in (0, 1)], axis=1)


def sweep_kernel(
    side, live_ref, pairs_hbm, parts_ref, red_real, last_ref, col_real, total_ref, red_ref, col_ref,
    out_ref, value_ref, rows, shift, seen, peak, mass, ta, tb, pairs_ref, sem,
):
    fetch = pltpu.make_async_copy(pairs_hbm, pairs_ref, sem)
    fetch.start()
    nred = red_ref.shape[0] // BLOCK
    ncol = col_ref.shape[0] // BLOCK
    value_ref[...] = merged(parts_ref[:, : 2 * nred, :]) if len(parts_ref.shape) == 3 else parts_ref[...]
    bias = jnp.where(by_block(red_real) > 0.0, -by_block(value_ref), very_low)
    hi = bias.astype(jnp.bfloat16).astype(jnp.float32)
    rest = bias - hi
    mid = rest.astype(jnp.bfloat16).astype(jnp.float32)
    low = rest - mid
    blank = jnp.zeros((DIM, BLOCK), jnp.float32)
    half = DIM // 2
    if nred < half:
        pad = jnp.zeros((half - nred, BLOCK), jnp.float32)
        hi, mid, low = (jnp.concatenate([v, pad], axis=0) for v in (hi, mid, low))
    ta[...] = jnp.concatenate([blank, hi, mid], axis=0).T.astype(jnp.bfloat16)
    tb[...] = jnp.concatenate([low, blank, blank[:half]], axis=0).T.astype(jnp.bfloat16)
    lane = lax.broadcasted_iota(jnp.int32, (1, LANES), 1)
    real = by_block(col_real) > 0.0
    shift[...] = jnp.where(real, by_block(last_ref), 0.0)
    seen[...] = jnp.zeros(seen.shape, jnp.float32)
    mass[...] = jnp.zeros(mass.shape, jnp.float32)
    fetch.wait()
    live = live_ref[0, 0]

    def scores(t):
        red = pairs_ref[side, t]
        col = pairs_ref[1 - side, t]
        one_a = ((lane == DIM + red) | (lane == DIM + half + red)).astype(jnp.float32).astype(jnp.bfloat16)
        one_b = (lane == red).astype(jnp.float32).astype(jnp.bfloat16)
        lhs = red_ref[pl.ds(pl.multiple_of(red * BLOCK, BLOCK), BLOCK), :] + ta[...]
        rhs = col_ref[pl.ds(pl.multiple_of(col * BLOCK, BLOCK), BLOCK), :] + one_a
        lhs = jnp.concatenate([lhs, tb[...]], axis=1)
        rhs = jnp.concatenate([rhs, jnp.broadcast_to(one_b, (BLOCK, LANES))], axis=1)
        score = lax.dot_general(lhs, rhs, (((1,), (1,)), ((), ())), preferred_element_type=jnp.float32)
        return score.reshape(BLOCK // 8, 8, BLOCK), col, jnp.where(t < live, col, ncol)

    def tile(t):
        score, col, slot = scores(t)
        terms = jnp.exp2((score - shift[pl.ds(col, 1), :][None]) * SCALE)
        mass[slot] = mass[slot] + jnp.sum(terms, axis=0)
        seen[pl.ds(slot, 1), :] = jnp.ones((1, LANES), jnp.float32)

    def group(i, _):
        for u in range(GROUP):
            tile(i * GROUP + u)
        return 0

    lax.fori_loop(0, (live + GROUP - 1) // GROUP, group, 0)

    def finish(part):
        for h in (0, 1):
            rows[pl.ds(h, ncol, stride=2), :] = part[:, h * LANES : (h + 1) * LANES]
        copies, height, _ = out_ref.shape
        out_ref[:, : 2 * ncol, :] = jnp.broadcast_to(rows[...][None], (copies, 2 * ncol, LANES))
        if height > 2 * ncol:
            out_ref[:, 2 * ncol :, :] = jnp.broadcast_to(total_ref[...][None], (copies, height - 2 * ncol, LANES))

    total = jnp.sum(mass[:ncol], axis=1)
    good = (total > 1e-27) & (total < 1e30)
    finish(jnp.where(good, shift[...] + jnp.log2(jnp.where(good, total, 1.0)) * INV_SCALE, very_low))
    used = jnp.concatenate([seen[:ncol, :]] * 2, axis=1) > 0.0
    lost = jnp.max(jnp.where(used & real & jnp.logical_not(good), 1.0, 0.0))

    @pl.when(lost > 0.0)
    def _():
        peak[...] = jnp.full(peak.shape, very_low, jnp.float32)
        mass[...] = jnp.zeros(mass.shape, jnp.float32)

        def exact(t, _):
            score, _, slot = scores(t)
            old = peak[slot]
            new = jnp.maximum(old, jnp.max(score, axis=0))
            terms = jnp.exp2((score - new[None]) * SCALE)
            mass[slot] = mass[slot] * jnp.exp2((old - new) * SCALE) + jnp.sum(terms, axis=0)
            peak[slot] = new
            return 0

        lax.fori_loop(0, live, exact, 0)
        tops = peak[:ncol]
        top = jnp.max(tops, axis=1, keepdims=True)
        total = jnp.sum(mass[:ncol] * jnp.exp2((tops - top) * SCALE), axis=1)
        some = total > 0.0
        finish(
            jnp.where(
                some, top.reshape(ncol, BLOCK) + jnp.log2(jnp.where(some, total, 1.0)) * INV_SCALE, very_low
            )
        )


def sweep(side, out, live, pairs, parts, red_real, last, col_real, total, red, col):
    nred, ncol = red.shape[0] // BLOCK, col.shape[0] // BLOCK
    return pl.pallas_call(
        functools.partial(sweep_kernel, side),
        out_shape=(
            jax.ShapeDtypeStruct(out, jnp.float32),
            jax.ShapeDtypeStruct((2 * nred, LANES), jnp.float32),
        ),
        in_specs=[SMEM, HBM] + [VMEM] * 7,
        out_specs=(VMEM, VMEM),
        scratch_shapes=[
            pltpu.VMEM((2 * ncol, LANES), jnp.float32),
            pltpu.VMEM((ncol, BLOCK), jnp.float32),
            pltpu.VMEM((ncol + 8, LANES), jnp.float32),
            pltpu.VMEM((ncol + 1, 8, BLOCK), jnp.float32),
            pltpu.VMEM((ncol + 1, 8, BLOCK), jnp.float32),
            pltpu.VMEM((BLOCK, LANES), jnp.bfloat16),
            pltpu.VMEM((BLOCK, LANES), jnp.bfloat16),
            pltpu.SMEM(pairs.shape, jnp.int32),
            pltpu.SemaphoreType.DMA,
        ],
        compiler_params=PARAMS,
    )(live, *in_hbm(pairs), parts, red_real, last, col_real, total, red, col)


def relay_kernel(rows, parts_ref, out_ref):
    copies, height, _ = out_ref.shape
    out_ref[:, :rows, :] = jnp.broadcast_to(merged(parts_ref[:, :rows, :])[None], (copies, rows, LANES))
    if height > rows:
        count = jnp.sum(parts_ref[:, rows:, :], axis=0)
        out_ref[:, rows:, :] = jnp.broadcast_to(count[None], (copies, height - rows, LANES))


def relay(rows, copies, parts):
    return pl.pallas_call(
        functools.partial(relay_kernel, rows),
        out_shape=jax.ShapeDtypeStruct((copies,) + parts.shape[1:], jnp.float32),
        in_specs=[VMEM],
        out_specs=VMEM,
        compiler_params=PARAMS,
    )(parts)


def finish_kernel(
    src_value, src_half, src_real, tgt_parts, tgt_half, tgt_real, first_src, first_tgt, src_out, tgt_out
):
    log_tgt = jnp.log(jnp.sum(first_src[:, src_half.shape[0] :, :], axis=0)[:1])
    log_src = jnp.log(jnp.sum(first_tgt[:, tgt_half.shape[0] :, :], axis=0)[:1])
    src_shift = -epsilon * (ITERS * log_src - (ITERS - 1) * log_tgt)
    tgt_shift = epsilon * ITERS * (log_src - log_tgt)
    for half, value, shift, real, out in (
        (src_half, src_value[...], src_shift, src_real, src_out),
        (tgt_half, merged(tgt_parts[...]), tgt_shift, tgt_real, tgt_out),
    ):
        out[...] = jnp.where(real[...] > 0.0, (half[...] - value) * (2.0 / DIM) + shift, 0.0)


def finish(src_value, src_half, src_real, tgt_parts, tgt_half, tgt_real, first_src, first_tgt):
    return pl.pallas_call(
        finish_kernel,
        out_shape=(
            jax.ShapeDtypeStruct(src_half.shape, jnp.float32),
            jax.ShapeDtypeStruct(tgt_half.shape, jnp.float32),
        ),
        in_specs=[VMEM] * 8,
        out_specs=(VMEM, VMEM),
        compiler_params=PARAMS,
    )(src_value, src_half, src_real, tgt_parts, tgt_half, tgt_real, first_src, first_tgt)


def on_device(sizes, src_points, tgt_points, src_counts, tgt_counts, tile_list, tile_count):
    pairs = tile_list.reshape(tile_list.shape[2:]).T
    src, tgt, src_half, tgt_half, src_real, tgt_real, src_total, tgt_total = prepare(
        src_counts, tgt_counts, src_points.T, tgt_points.T
    )
    src_rows = src_half.shape[0]
    tgt_rows = tgt_half.shape[0]

    tgt_parts = tgt_half
    src_value = src_half
    first = []
    for step in range(ITERS):
        extra = src_total.shape[0] if step == 0 else 0
        out = (sizes["y"], src_rows + extra, LANES)
        src_parts, tgt_value = sweep(
            1, out, tile_count, pairs, tgt_parts, tgt_real, src_value, src_real, tgt_total, tgt, src
        )
        src_parts = lax.all_to_all(src_parts, "y", 0, 0)
        out = (sizes["z"], tgt_rows + extra, LANES)
        tgt_parts, src_value = sweep(
            0, out, tile_count, pairs, src_parts, src_real, tgt_value, tgt_real, src_total, src, tgt
        )
        tgt_parts = lax.all_to_all(tgt_parts, "z", 0, 0)
        tgt_parts = relay(tgt_rows, sizes["x"] * sizes["core"], tgt_parts)
        tgt_parts = lax.all_to_all(tgt_parts, ("x", "core"), 0, 0)
        if step == 0:
            first = [src_parts, tgt_parts]
    src_out, tgt_out = finish(src_value, src_half, src_real, tgt_parts, tgt_half, tgt_real, *first)
    return (src_out.reshape(-1), tgt_out.reshape(-1))


def solution(mesh):
    sizes = {"x": 4, "z": 8, "core": 2, "y": mesh.shape["col"]}
    fine = Mesh(mesh.devices.reshape(tuple(sizes.values())), tuple(sizes))
    row = ("x", "z", "core")
    return jax.shard_map(
        functools.partial(on_device, sizes),
        mesh=fine,
        in_specs=(P(row, None), P("y", None), P(row), P("y"), P(row, "y", None, None), P(row, "y")),
        out_specs=(P(row), P("y")),
        check_vma=False,
    )
```

time: 158 us -> 157 us (level)
  blocking collectives: 104 us -> 135 us
  starting transfers between devices: 12.9 us -> 0 us
  waiting for transfers between devices: 12.7 us -> 0 us
  Pallas kernels: 22.8 us -> 19.6 us
  other arithmetic: 2.59 us -> 0 us
    all_to_all x2 -> x3, blocking collectives: 32.2 us -> 51.2 us  [on_device(): tgt_parts = lax.all_to_all(tgt_parts, 'z', 0, 0)]
    all_to_all x2 -> x3, blocking collectives: 32 us -> 50.3 us  [on_device(): tgt_parts = lax.all_to_all(tgt_parts, ('x', 'core'), 0, 0)]
    all_to_all x2 -> x0, starting transfers between devices: 12.9 us -> none  [the longest x1 7.49 us: on_device(): tgt_parts = lax.all_to_all(tgt_parts, ('x', 'core'), 0, 0)]
    all_to_all x2 -> x0, waiting for transfers between devices: 12.7 us -> none  [the longest x1 6.81 us: on_device(): tgt_parts = lax.all_to_all(tgt_parts, 'z', 0, 0)]
    all_to_all x3, blocking collectives: 39.4 us -> 33.6 us  [on_device(): src_parts = lax.all_to_all(src_parts, 'y', 0, 0)]
    pallas_call x6 -> x7, Pallas kernels: 19.8 us -> 17.3 us  [the longest x6 16.6 us: sweep(): pl.pallas_call(functools.partial(sweep_kernel, side), out_shape=(jax.Shap...]
  transfers between devices with their start and end apart: 2 -> 0, of which waited for: 2 -> 0; matrix products, arithmetic and copies ran while one was open for 1% -> 0% of each run, Pallas kernels for 0% -> 0%
where the time goes in v4:
time: 157 us; the launch traced here: 156 us
  blocking collectives  135 us (86%)
  Pallas kernels  19.6 us (12%)
    all_to_all x3, blocking collectives, on_device(): tgt_parts = lax.all_to_all(tgt_parts, 'z', 0, 0)  51.2 us
    all_to_all x3, blocking collectives, on_device(): tgt_parts = lax.all_to_all(tgt_parts, ('x', 'core'), 0, 0)  50.3 us
    all_to_all x3, blocking collectives, on_device(): src_parts = lax.all_to_all(src_parts, 'y', 0, 0)  33.6 us
    pallas_call x6, Pallas kernels, sweep(): pl.pallas_call(functools.partial(sweep_kernel, side), out_shape=(jax.Shap...  16.6 us

profile of v4, /device:TPU:1, one launch (start us, length us, event | category | flops | bytes accessed | tf_op | source)
XLA Modules:
  0.0 156.0 jit_solution(14291691123123000645)
XLA Ops:
  1.3 2.1 %shard_map.77 = (bf16[4096,128]{1,0:T(8,128)(2,1)S(1)}, bf16[8192,128]{1,0:T(8,128)(2,1)S(1)}, f32[32,128]{1,0:T(8,128)S(1)}, f32[64,128]{1,0:T(8,128)S(1)}, f32...) custom-call(s32[16]{0:T(128)} %counts_s.1, s32[32]{0:T(128)} %counts_t.1, ...), custom_call_target="tpu_custom_call" | custom-call | tf_op jit(solution)/shard_map/pallas_call | solution.py:67
  3.4 6.8 %shard_map.78 = (f32[8,40,128]{2,1,0:T(8,128)S(1)}, f32[64,128]{1,0:T(8,128)S(1)}) custom-call(s32[1,1]{1,0:T(1,128)S(6)} %copy.8.live_ref, s32[2,48]{1,0:T(2,128)} %bitcast.9, f32[64,128]{1,0:T(8,128)S(1)} %get-tuple-element.24.parts_ref.tgt_half, f32[64,128]{1,0:T(8,128)S(1)} %get-tuple-element.25.red_real.col_real.tgt_real, ...), custom_call_target="tpu_custom_call" | custom-call | tf_op jit(solution)/shard_map/pallas_call | solution.py:193
  10.2 12.0 %all_to_all.45.parts_ref.first_src = f32[8,40,128]{2,1,0:T(8,128)S(1)} all-to-all(f32[8,40,128]{2,1,0:T(8,128)S(1)} %get-tuple-element.31), channel_id=1, replica_groups=mesh['x'=4,'z'=8,'core'=2,'y'=8] {'y'}, dimensions={0} | all-to-all | bytes 327680 | tf_op jit(solution)/shard_map/all_to_all | solution.py:278
  22.2 2.0 %shard_map.79 = (f32[8,72,128]{2,1,0:T(8,128)S(1)}, f32[32,128]{1,0:T(8,128)S(1)}) custom-call(s32[1,1]{1,0:T(1,128)S(6)} %copy.8.live_ref, s32[2,48]{1,0:T(2,128)} %bitcast.10, f32[8,40,128]{2,1,0:T(8,128)S(1)} %all_to_all.45.parts_ref.first_src, f32[32,128]{1,0:T(8,128)S(1)} %get-tuple-element.27.col_real.red_real.src_real, ...), custom_call_target="tpu_custom_call" | custom-call | tf_op jit(solution)/shard_map/pallas_call | solution.py:193
  24.2 25.9 %all_to_all.46.parts_ref = f32[8,72,128]{2,1,0:T(8,128)S(1)} all-to-all(f32[8,72,128]{2,1,0:T(8,128)S(1)} %get-tuple-element.34), channel_id=1, replica_groups=mesh['x'=4,'z'=8,'core'=2,'y'=8] {'z'}, dimensions={0} | all-to-all | bytes 589824 | tf_op jit(solution)/shard_map/all_to_all | solution.py:283
  50.0 0.1 shard_map.80
  50.1 18.2 %all_to_all.47.parts_ref.first_tgt = f32[8,72,128]{2,1,0:T(8,128)S(1)} all-to-all(f32[8,72,128]{2,1,0:T(8,128)S(1)} %shard_map.80), channel_id=1, replica_groups=mesh['x'=4,'z'=8,'core'=2,'y'=8] {'x','core'}, dimensions={0} | all-to-all | bytes 589824 | tf_op jit(solution)/shard_map/all_to_all | solution.py:285
  68.3 1.9 %shard_map.81 = (f32[8,32,128]{2,1,0:T(8,128)S(1)}, f32[64,128]{1,0:T(8,128)S(1)}) custom-call(s32[1,1]{1,0:T(1,128)S(6)} %copy.8.live_ref, s32[2,48]{1,0:T(2,128)} %bitcast.11, f32[8,72,128]{2,1,0:T(8,128)S(1)} %all_to_all.47.parts_ref.first_tgt, f32[64,128]{1,0:T(8,128)S(1)} %get-tuple-element.25.red_real.col_real.tgt_real, ...), custom_call_target="tpu_custom_call" | custom-call | tf_op jit(solution)/shard_map/pallas_call | solution.py:193
  70.2 10.9 %all_to_all.48.parts_ref = f32[8,32,128]{2,1,0:T(8,128)S(1)} all-to-all(f32[8,32,128]{2,1,0:T(8,128)S(1)} %get-tuple-element.36), channel_id=1, replica_groups=mesh['x'=4,'z'=8,'core'=2,'y'=8] {'y'}, dimensions={0} | all-to-all | bytes 262144 | tf_op jit(solution)/shard_map/all_to_all | solution.py:278
  81.1 2.0 %shard_map.82 = (f32[8,64,128]{2,1,0:T(8,128)S(1)}, f32[32,128]{1,0:T(8,128)S(1)}) custom-call(s32[1,1]{1,0:T(1,128)S(6)} %copy.8.live_ref, s32[2,48]{1,0:T(2,128)} %bitcast.12, f32[8,32,128]{2,1,0:T(8,128)S(1)} %all_to_all.48.parts_ref, f32[32,128]{1,0:T(8,128)S(1)} %get-tuple-element.27.col_real.red_real.src_real, ...), custom_call_target="tpu_custom_call" | custom-call | tf_op jit(solution)/shard_map/pallas_call | solution.py:193
  83.1 12.2 %all_to_all.49.parts_ref = f32[8,64,128]{2,1,0:T(8,128)S(1)} all-to-all(f32[8,64,128]{2,1,0:T(8,128)S(1)} %get-tuple-element.38), channel_id=1, replica_groups=mesh['x'=4,'z'=8,'core'=2,'y'=8] {'z'}, dimensions={0} | all-to-all | bytes 524288 | tf_op jit(solution)/shard_map/all_to_all | solution.py:283
  95.3 0.1 shard_map.83
  95.3 16.4 %all_to_all.50.parts_ref = f32[8,64,128]{2,1,0:T(8,128)S(1)} all-to-all(f32[8,64,128]{2,1,0:T(8,128)S(1)} %shard_map.83), channel_id=1, replica_groups=mesh['x'=4,'z'=8,'core'=2,'y'=8] {'x','core'}, dimensions={0} | all-to-all | bytes 524288 | tf_op jit(solution)/shard_map/all_to_all | solution.py:285
  111.7 1.9 %shard_map.84 = (f32[8,32,128]{2,1,0:T(8,128)S(1)}, f32[64,128]{1,0:T(8,128)S(1)}) custom-call(s32[1,1]{1,0:T(1,128)S(6)} %copy.8.live_ref, s32[2,48]{1,0:T(2,128)} %bitcast.13, f32[8,64,128]{2,1,0:T(8,128)S(1)} %all_to_all.50.parts_ref, f32[64,128]{1,0:T(8,128)S(1)} %get-tuple-element.25.red_real.col_real.tgt_real, ...), custom_call_target="tpu_custom_call" | custom-call | tf_op jit(solution)/shard_map/pallas_call | solution.py:193
  113.6 10.6 %all_to_all.51.parts_ref = f32[8,32,128]{2,1,0:T(8,128)S(1)} all-to-all(f32[8,32,128]{2,1,0:T(8,128)S(1)} %get-tuple-element.40), channel_id=1, replica_groups=mesh['x'=4,'z'=8,'core'=2,'y'=8] {'y'}, dimensions={0} | all-to-all | bytes 262144 | tf_op jit(solution)/shard_map/all_to_all | solution.py:278
  124.2 2.0 %shard_map.85 = (f32[8,64,128]{2,1,0:T(8,128)S(1)}, f32[32,128]{1,0:T(8,128)S(1)}) custom-call(s32[1,1]{1,0:T(1,128)S(6)} %copy.8.live_ref, s32[2,48]{1,0:T(2,128)} %bitcast.14, f32[8,32,128]{2,1,0:T(8,128)S(1)} %all_to_all.51.parts_ref, f32[32,128]{1,0:T(8,128)S(1)} %get-tuple-element.27.col_real.red_real.src_real, ...), custom_call_target="tpu_custom_call" | custom-call | tf_op jit(solution)/shard_map/pallas_call | solution.py:193
  126.3 13.2 %all_to_all.52.parts_ref = f32[8,64,128]{2,1,0:T(8,128)S(1)} all-to-all(f32[8,64,128]{2,1,0:T(8,128)S(1)} %get-tuple-element.43), channel_id=1, replica_groups=mesh['x'=4,'z'=8,'core'=2,'y'=8] {'z'}, dimensions={0} | all-to-all | bytes 524288 | tf_op jit(solution)/shard_map/all_to_all | solution.py:283
  139.5 0.1 shard_map.86
  139.5 15.7 %all_to_all.53.tgt_parts = f32[8,64,128]{2,1,0:T(8,128)S(1)} all-to-all(f32[8,64,128]{2,1,0:T(8,128)S(1)} %shard_map.86), channel_id=1, replica_groups=mesh['x'=4,'z'=8,'core'=2,'y'=8] {'x','core'}, dimensions={0} | all-to-all | bytes 524288 | tf_op jit(solution)/shard_map/all_to_all | solution.py:285
  155.3 0.7 shard_map.87

commit v5 on v4

--- a/solution.py
+++ b/solution.py
@@ -11,7 +11,8 @@
 BLOCK = 256
 ITERS = 3
 LANES = 128
-GROUP = 16
+GROUP = 48
+PART = 16
 
 epsilon = 0.05
 very_low = -1e30
@@ -35,10 +36,10 @@
     return top + jnp.log2(total) * INV_SCALE
 
 
-def prepare_kernel(counts_s, counts_t, src_t, tgt_t, src, tgt, half_s, half_t, real_s, real_t, sum_s, sum_t, cs, ct, xs, xt, sems):
+def prepare_kernel(counts_s, counts_t, src_t, tgt_t, pairs_in, src, tgt, half_s, half_t, real_s, real_t, sum_s, sum_t, pairs_out, xs, xt, cs, ct, sems):
     copies = [
         pltpu.make_async_copy(a, b, sems.at[i])
-        for i, (a, b) in enumerate(((counts_s, cs), (src_t, xs), (counts_t, ct), (tgt_t, xt)))
+        for i, (a, b) in enumerate(((counts_s, cs), (src_t, xs), (counts_t, ct), (tgt_t, xt), (pairs_in, pairs_out)))
     ]
     for copy in copies:
         copy.start()
@@ -57,9 +58,10 @@
             out[row * LANES : (row + 1) * LANES, :] = chunk.T.astype(jnp.bfloat16)
             slot = lane + (row % 2) * LANES
             real[row : row + 1, :] = (slot < counts[row // 2]).astype(jnp.float32)
-
-
-def prepare(src_counts, tgt_counts, src_t, tgt_t):
+    copies[4].wait()
+
+
+def prepare(src_counts, tgt_counts, src_t, tgt_t, pairs):
     ns, nt = src_t.shape[1], tgt_t.shape[1]
     rows_s = jax.ShapeDtypeStruct((ns // LANES, LANES), jnp.float32)
     rows_t = jax.ShapeDtypeStruct((nt // LANES, LANES), jnp.float32)
@@ -75,18 +77,26 @@
             rows_t,
             total,
             total,
+            jax.ShapeDtypeStruct(pairs.shape, jnp.int32),
+            jax.ShapeDtypeStruct(src_t.shape, jnp.bfloat16),
+            jax.ShapeDtypeStruct(tgt_t.shape, jnp.bfloat16),
         ),
-        in_specs=[HBM] * 4,
-        out_specs=(VMEM,) * 8,
+        in_specs=[HBM] * 5,
+        out_specs=(VMEM,) * 11,
         scratch_shapes=[
             pltpu.SMEM(src_counts.shape, jnp.int32),
             pltpu.SMEM(tgt_counts.shape, jnp.int32),
-            pltpu.VMEM(src_t.shape, jnp.bfloat16),
-            pltpu.VMEM(tgt_t.shape, jnp.bfloat16),
-            pltpu.SemaphoreType.DMA((4,)),
+            pltpu.SemaphoreType.DMA((5,)),
         ],
         compiler_params=PARAMS,
-    )(*in_hbm(src_counts, tgt_counts, src_t, tgt_t))
+    )(*in_hbm(src_counts, tgt_counts, src_t, tgt_t, pairs))
+
+
+def split(value):
+    hi = value.astype(jnp.bfloat16).astype(jnp.float32)
+    rest = value - hi
+    mid = rest.astype(jnp.bfloat16).astype(jnp.float32)
+    return hi, mid, rest - mid
 
 
 def by_block(rows_ref):
@@ -96,28 +106,31 @@
 
 def sweep_kernel(
     side, live_ref, pairs_hbm, parts_ref, red_real, last_ref, col_real, total_ref, red_ref, col_ref,
-    out_ref, value_ref, rows, shift, seen, peak, mass, ta, tb, pairs_ref, sem,
+    out_ref, value_ref, rows, shift, seen, peak, mass, columns, shifts, pairs_ref, sem,
 ):
     fetch = pltpu.make_async_copy(pairs_hbm, pairs_ref, sem)
     fetch.start()
     nred = red_ref.shape[0] // BLOCK
-    ncol = col_ref.shape[0] // BLOCK
+    ncol = col_ref.shape[1] // BLOCK
     value_ref[...] = merged(parts_ref[:, : 2 * nred, :]) if len(parts_ref.shape) == 3 else parts_ref[...]
     bias = jnp.where(by_block(red_real) > 0.0, -by_block(value_ref), very_low)
-    hi = bias.astype(jnp.bfloat16).astype(jnp.float32)
-    rest = bias - hi
-    mid = rest.astype(jnp.bfloat16).astype(jnp.float32)
-    low = rest - mid
-    blank = jnp.zeros((DIM, BLOCK), jnp.float32)
-    half = DIM // 2
-    if nred < half:
-        pad = jnp.zeros((half - nred, BLOCK), jnp.float32)
-        hi, mid, low = (jnp.concatenate([v, pad], axis=0) for v in (hi, mid, low))
-    ta[...] = jnp.concatenate([blank, hi, mid], axis=0).T.astype(jnp.bfloat16)
-    tb[...] = jnp.concatenate([low, blank, blank[:half]], axis=0).T.astype(jnp.bfloat16)
-    lane = lax.broadcasted_iota(jnp.int32, (1, LANES), 1)
+    hi, mid, low = split(bias)
+    for i in range(nred // PART):
+        own = slice(i * PART, (i + 1) * PART)
+        ones = (lax.broadcasted_iota(jnp.int32, (PART, BLOCK), 0) < 3).astype(jnp.float32)
+        pieces = [jnp.zeros((DIM, BLOCK), jnp.float32), hi[own], mid[own], low[own], ones]
+        columns[i] = jnp.concatenate(pieces, axis=0).T.astype(jnp.bfloat16)
+    lane = lax.broadcasted_iota(jnp.int32, (3 * PART, 1), 0)
     real = by_block(col_real) > 0.0
-    shift[...] = jnp.where(real, by_block(last_ref), 0.0)
+    last = jnp.where(real, by_block(last_ref), 0.0)
+    shift[...] = last
+    lower = split(-last)
+    row = lax.broadcasted_iota(jnp.int32, (PART, BLOCK), 0)
+    for c in range(ncol):
+        chunk = jnp.zeros((PART, BLOCK), jnp.float32)
+        for i in range(3):
+            chunk = jnp.where(row == i, lower[i][c : c + 1, :], chunk)
+        shifts[c] = chunk.astype(jnp.bfloat16)
     seen[...] = jnp.zeros(seen.shape, jnp.float32)
     mass[...] = jnp.zeros(mass.shape, jnp.float32)
     fetch.wait()
@@ -126,18 +139,18 @@
     def scores(t):
         red = pairs_ref[side, t]
         col = pairs_ref[1 - side, t]
-        one_a = ((lane == DIM + red) | (lane == DIM + half + red)).astype(jnp.float32).astype(jnp.bfloat16)
-        one_b = (lane == red).astype(jnp.float32).astype(jnp.bfloat16)
-        lhs = red_ref[pl.ds(pl.multiple_of(red * BLOCK, BLOCK), BLOCK), :] + ta[...]
-        rhs = col_ref[pl.ds(pl.multiple_of(col * BLOCK, BLOCK), BLOCK), :] + one_a
-        lhs = jnp.concatenate([lhs, tb[...]], axis=1)
-        rhs = jnp.concatenate([rhs, jnp.broadcast_to(one_b, (BLOCK, LANES))], axis=1)
-        score = lax.dot_general(lhs, rhs, (((1,), (1,)), ((), ())), preferred_element_type=jnp.float32)
+        place = lane - (red & (PART - 1))
+        ones = ((place == 0) | (place == PART) | (place == 2 * PART)).astype(jnp.float32).astype(jnp.bfloat16)
+        ones = jnp.broadcast_to(ones, (3 * PART, BLOCK))
+        lhs = red_ref[pl.ds(pl.multiple_of(red * BLOCK, BLOCK), BLOCK), :] + columns[red // PART]
+        rhs = col_ref[:, pl.ds(pl.multiple_of(col * BLOCK, BLOCK), BLOCK)]
+        rhs = jnp.concatenate([rhs, ones, shifts[col]], axis=0)
+        score = jnp.dot(lhs, rhs, preferred_element_type=jnp.float32)
         return score.reshape(BLOCK // 8, 8, BLOCK), col, jnp.where(t < live, col, ncol)
 
     def tile(t):
         score, col, slot = scores(t)
-        terms = jnp.exp2((score - shift[pl.ds(col, 1), :][None]) * SCALE)
+        terms = jnp.exp2(score * SCALE)
         mass[slot] = mass[slot] + jnp.sum(terms, axis=0)
         seen[pl.ds(slot, 1), :] = jnp.ones((1, LANES), jnp.float32)
 
@@ -183,20 +196,20 @@
         some = total > 0.0
         finish(
             jnp.where(
-                some, top.reshape(ncol, BLOCK) + jnp.log2(jnp.where(some, total, 1.0)) * INV_SCALE, very_low
+                some, shift[...] + top.reshape(ncol, BLOCK) + jnp.log2(jnp.where(some, total, 1.0)) * INV_SCALE, very_low
             )
         )
 
 
 def sweep(side, out, live, pairs, parts, red_real, last, col_real, total, red, col):
-    nred, ncol = red.shape[0] // BLOCK, col.shape[0] // BLOCK
+    nred, ncol = red.shape[0] // BLOCK, col.shape[1] // BLOCK
     return pl.pallas_call(
         functools.partial(sweep_kernel, side),
         out_shape=(
             jax.ShapeDtypeStruct(out, jnp.float32),
             jax.ShapeDtypeStruct((2 * nred, LANES), jnp.float32),
         ),
-        in_specs=[SMEM, HBM] + [VMEM] * 7,
+        in_specs=[SMEM] + [VMEM] * 8,
         out_specs=(VMEM, VMEM),
         scratch_shapes=[
             pltpu.VMEM((2 * ncol, LANES), jnp.float32),
@@ -204,13 +217,13 @@
             pltpu.VMEM((ncol + 8, LANES), jnp.float32),
             pltpu.VMEM((ncol + 1, 8, BLOCK), jnp.float32),
             pltpu.VMEM((ncol + 1, 8, BLOCK), jnp.float32),
-            pltpu.VMEM((BLOCK, LANES), jnp.bfloat16),
-            pltpu.VMEM((BLOCK, LANES), jnp.bfloat16),
+            pltpu.VMEM((nred // PART, BLOCK, LANES), jnp.bfloat16),
+            pltpu.VMEM((ncol, PART, BLOCK), jnp.bfloat16),
             pltpu.SMEM(pairs.shape, jnp.int32),
             pltpu.SemaphoreType.DMA,
         ],
         compiler_params=PARAMS,
-    )(live, *in_hbm(pairs), parts, red_real, last, col_real, total, red, col)
+    )(live, pairs, parts, red_real, last, col_real, total, red, col)
 
 
 def relay_kernel(rows, parts_ref, out_ref):
@@ -260,8 +273,8 @@
 
 def on_device(sizes, src_points, tgt_points, src_counts, tgt_counts, tile_list, tile_count):
     pairs = tile_list.reshape(tile_list.shape[2:]).T
-    src, tgt, src_half, tgt_half, src_real, tgt_real, src_total, tgt_total = prepare(
-        src_counts, tgt_counts, src_points.T, tgt_points.T
+    src, tgt, src_half, tgt_half, src_real, tgt_real, src_total, tgt_total, pairs, src_t, tgt_t = prepare(
+        src_counts, tgt_counts, src_points.T, tgt_points.T, pairs
     )
     src_rows = src_half.shape[0]
     tgt_rows = tgt_half.shape[0]
@@ -273,12 +286,12 @@
         extra = src_total.shape[0] if step == 0 else 0
         out = (sizes["y"], src_rows + extra, LANES)
         src_parts, tgt_value = sweep(
-            1, out, tile_count, pairs, tgt_parts, tgt_real, src_value, src_real, tgt_total, tgt, src
+            1, out, tile_count, pairs, tgt_parts, tgt_real, src_value, src_real, tgt_total, tgt, src_t
         )
         src_parts = lax.all_to_all(src_parts, "y", 0, 0)
         out = (sizes["z"], tgt_rows + extra, LANES)
         tgt_parts, src_value = sweep(
-            0, out, tile_count, pairs, src_parts, src_real, tgt_value, tgt_real, src_total, src, tgt
+            0, out, tile_count, pairs, src_parts, src_real, tgt_value, tgt_real, src_total, src, tgt_t
         )
         tgt_parts = lax.all_to_all(tgt_parts, "z", 0, 0)
         tgt_parts = relay(tgt_rows, sizes["x"] * sizes["core"], tgt_parts)

time: 157 us -> 159 us (1.013)
  blocking collectives: 135 us -> 137 us
    all_to_all x3, blocking collectives: 33.6 us -> 41.6 us  [on_device(): src_parts = lax.all_to_all(src_parts, 'y', 0, 0)]
    all_to_all x3, blocking collectives: 50.3 us -> 44.6 us  [on_device(): tgt_parts = lax.all_to_all(tgt_parts, ('x', 'core'), 0, 0)]
where the time goes in v5:
time: 159 us
  blocking collectives  137 us (86%)
  Pallas kernels  20.4 us (13%)
    all_to_all x3, blocking collectives, on_device(): tgt_parts = lax.all_to_all(tgt_parts, 'z', 0, 0)  50.7 us
    all_to_all x3, blocking collectives, on_device(): tgt_parts = lax.all_to_all(tgt_parts, ('x', 'core'), 0, 0)  44.6 us
    all_to_all x3, blocking collectives, on_device(): src_parts = lax.all_to_all(src_parts, 'y', 0, 0)  41.6 us
    pallas_call x6, Pallas kernels, sweep(): pl.pallas_call(functools.partial(sweep_kernel, side), out_shape=(jax.Shap...  17.4 us

profile of v5, /device:TPU:1, one launch (start us, length us, event | category | flops | bytes accessed | tf_op | source)
XLA Modules:
  0.0 158.6 jit_solution(11899817883038339721)
XLA Ops:
  1.3 2.1 %shard_map.77 = (bf16[4096,128]{1,0:T(8,128)(2,1)S(1)}, bf16[8192,128]{1,0:T(8,128)(2,1)S(1)}, f32[32,128]{1,0:T(8,128)S(1)}, f32[64,128]{1,0:T(8,128)S(1)}, f32...) custom-call(s32[16]{0:T(128)} %counts_s.1, ...), custom_call_target="tpu_custom_call" | custom-call | tf_op jit(solution)/shard_map/pallas_call | solution.py:69
  3.4 2.8 %shard_map.78 = (f32[8,40,128]{2,1,0:T(8,128)S(1)}, f32[64,128]{1,0:T(8,128)S(1)}) custom-call(s32[1,1]{1,0:T(1,128)S(6)} %copy.8.live_ref, s32[2,48]{1,0:T(2,128)S(1)} %get-tuple-element.27.pairs_hbm, f32[64,128]{1,0:T(8,128)S(1)} %get-tuple-element.28.parts_ref.tgt_half, f32[64,128]{1,0:T(8,128)S(1)} %get-tuple-element.29.red_real.col_real.tgt_real, ...), custom_call_target="tpu_custom_call" | custom-call | tf_op jit(solution)/shard_map/pallas_call | solution.py:206
  6.2 20.0 %all_to_all.45.parts_ref.first_src = f32[8,40,128]{2,1,0:T(8,128)S(1)} all-to-all(f32[8,40,128]{2,1,0:T(8,128)S(1)} %get-tuple-element.35), channel_id=1, replica_groups=mesh['x'=4,'z'=8,'core'=2,'y'=8] {'y'}, dimensions={0} | all-to-all | bytes 327680 | tf_op jit(solution)/shard_map/all_to_all | solution.py:291
  26.2 2.9 %shard_map.79 = (f32[8,72,128]{2,1,0:T(8,128)S(1)}, f32[32,128]{1,0:T(8,128)S(1)}) custom-call(s32[1,1]{1,0:T(1,128)S(6)} %copy.8.live_ref, s32[2,48]{1,0:T(2,128)S(1)} %get-tuple-element.27.pairs_hbm, f32[8,40,128]{2,1,0:T(8,128)S(1)} %all_to_all.45.parts_ref.first_src, f32[32,128]{1,0:T(8,128)S(1)} %get-tuple-element.31.col_real.red_real.src_real, ...), custom_call_target="tpu_custom_call" | custom-call | tf_op jit(solution)/shard_map/pallas_call | solution.py:206
  29.1 20.6 %all_to_all.46.parts_ref = f32[8,72,128]{2,1,0:T(8,128)S(1)} all-to-all(f32[8,72,128]{2,1,0:T(8,128)S(1)} %get-tuple-element.40), channel_id=1, replica_groups=mesh['x'=4,'z'=8,'core'=2,'y'=8] {'z'}, dimensions={0} | all-to-all | bytes 589824 | tf_op jit(solution)/shard_map/all_to_all | solution.py:296
  49.7 0.1 shard_map.80
  49.8 15.3 %all_to_all.47.parts_ref.first_tgt = f32[8,72,128]{2,1,0:T(8,128)S(1)} all-to-all(f32[8,72,128]{2,1,0:T(8,128)S(1)} %shard_map.80), channel_id=1, replica_groups=mesh['x'=4,'z'=8,'core'=2,'y'=8] {'x','core'}, dimensions={0} | all-to-all | bytes 589824 | tf_op jit(solution)/shard_map/all_to_all | solution.py:298
  65.1 2.8 %shard_map.81 = (f32[8,32,128]{2,1,0:T(8,128)S(1)}, f32[64,128]{1,0:T(8,128)S(1)}) custom-call(s32[1,1]{1,0:T(1,128)S(6)} %copy.8.live_ref, s32[2,48]{1,0:T(2,128)S(1)} %get-tuple-element.27.pairs_hbm, f32[8,72,128]{2,1,0:T(8,128)S(1)} %all_to_all.47.parts_ref.first_tgt, f32[64,128]{1,0:T(8,128)S(1)} %get-tuple-element.29.red_real.col_real.tgt_real, ...), custom_call_target="tpu_custom_call" | custom-call | tf_op jit(solution)/shard_map/pallas_call | solution.py:206
  68.0 10.4 %all_to_all.48.parts_ref = f32[8,32,128]{2,1,0:T(8,128)S(1)} all-to-all(f32[8,32,128]{2,1,0:T(8,128)S(1)} %get-tuple-element.42), channel_id=1, replica_groups=mesh['x'=4,'z'=8,'core'=2,'y'=8] {'y'}, dimensions={0} | all-to-all | bytes 262144 | tf_op jit(solution)/shard_map/all_to_all | solution.py:291
  78.4 3.1 %shard_map.82 = (f32[8,64,128]{2,1,0:T(8,128)S(1)}, f32[32,128]{1,0:T(8,128)S(1)}) custom-call(s32[1,1]{1,0:T(1,128)S(6)} %copy.8.live_ref, s32[2,48]{1,0:T(2,128)S(1)} %get-tuple-element.27.pairs_hbm, f32[8,32,128]{2,1,0:T(8,128)S(1)} %all_to_all.48.parts_ref, f32[32,128]{1,0:T(8,128)S(1)} %get-tuple-element.31.col_real.red_real.src_real, ...), custom_call_target="tpu_custom_call" | custom-call | tf_op jit(solution)/shard_map/pallas_call | solution.py:206
  81.5 15.4 %all_to_all.49.parts_ref = f32[8,64,128]{2,1,0:T(8,128)S(1)} all-to-all(f32[8,64,128]{2,1,0:T(8,128)S(1)} %get-tuple-element.44), channel_id=1, replica_groups=mesh['x'=4,'z'=8,'core'=2,'y'=8] {'z'}, dimensions={0} | all-to-all | bytes 524288 | tf_op jit(solution)/shard_map/all_to_all | solution.py:296
  96.9 0.1 shard_map.83
  97.0 14.6 %all_to_all.50.parts_ref = f32[8,64,128]{2,1,0:T(8,128)S(1)} all-to-all(f32[8,64,128]{2,1,0:T(8,128)S(1)} %shard_map.83), channel_id=1, replica_groups=mesh['x'=4,'z'=8,'core'=2,'y'=8] {'x','core'}, dimensions={0} | all-to-all | bytes 524288 | tf_op jit(solution)/shard_map/all_to_all | solution.py:298
  111.6 2.8 %shard_map.84 = (f32[8,32,128]{2,1,0:T(8,128)S(1)}, f32[64,128]{1,0:T(8,128)S(1)}) custom-call(s32[1,1]{1,0:T(1,128)S(6)} %copy.8.live_ref, s32[2,48]{1,0:T(2,128)S(1)} %get-tuple-element.27.pairs_hbm, f32[8,64,128]{2,1,0:T(8,128)S(1)} %all_to_all.50.parts_ref, f32[64,128]{1,0:T(8,128)S(1)} %get-tuple-element.29.red_real.col_real.tgt_real, ...), custom_call_target="tpu_custom_call" | custom-call | tf_op jit(solution)/shard_map/pallas_call | solution.py:206
  114.5 11.2 %all_to_all.51.parts_ref = f32[8,32,128]{2,1,0:T(8,128)S(1)} all-to-all(f32[8,32,128]{2,1,0:T(8,128)S(1)} %get-tuple-element.46), channel_id=1, replica_groups=mesh['x'=4,'z'=8,'core'=2,'y'=8] {'y'}, dimensions={0} | all-to-all | bytes 262144 | tf_op jit(solution)/shard_map/all_to_all | solution.py:291
  125.6 2.9 %shard_map.85 = (f32[8,64,128]{2,1,0:T(8,128)S(1)}, f32[32,128]{1,0:T(8,128)S(1)}) custom-call(s32[1,1]{1,0:T(1,128)S(6)} %copy.8.live_ref, s32[2,48]{1,0:T(2,128)S(1)} %get-tuple-element.27.pairs_hbm, f32[8,32,128]{2,1,0:T(8,128)S(1)} %all_to_all.51.parts_ref, f32[32,128]{1,0:T(8,128)S(1)} %get-tuple-element.31.col_real.red_real.src_real, ...), custom_call_target="tpu_custom_call" | custom-call | tf_op jit(solution)/shard_map/pallas_call | solution.py:206
  128.6 14.6 %all_to_all.52.parts_ref = f32[8,64,128]{2,1,0:T(8,128)S(1)} all-to-all(f32[8,64,128]{2,1,0:T(8,128)S(1)} %get-tuple-element.49), channel_id=1, replica_groups=mesh['x'=4,'z'=8,'core'=2,'y'=8] {'z'}, dimensions={0} | all-to-all | bytes 524288 | tf_op jit(solution)/shard_map/all_to_all | solution.py:296
  143.2 0.1 shard_map.86
  143.3 14.7 %all_to_all.53.tgt_parts = f32[8,64,128]{2,1,0:T(8,128)S(1)} all-to-all(f32[8,64,128]{2,1,0:T(8,128)S(1)} %shard_map.86), channel_id=1, replica_groups=mesh['x'=4,'z'=8,'core'=2,'y'=8] {'x','core'}, dimensions={0} | all-to-all | bytes 524288 | tf_op jit(solution)/shard_map/all_to_all | solution.py:298
  157.9 0.7 shard_map.87

commit v6 on v5

--- a/solution.py
+++ b/solution.py
@@ -11,8 +11,9 @@
 BLOCK = 256
 ITERS = 3
 LANES = 128
-GROUP = 48
 PART = 16
+TILE_BITS = 8
+TILE_BASE = 1 << TILE_BITS
 
 epsilon = 0.05
 very_low = -1e30
@@ -36,10 +37,10 @@
     return top + jnp.log2(total) * INV_SCALE
 
 
-def prepare_kernel(counts_s, counts_t, src_t, tgt_t, pairs_in, src, tgt, half_s, half_t, real_s, real_t, sum_s, sum_t, pairs_out, xs, xt, cs, ct, sems):
+def prepare_kernel(counts_s, counts_t, src_t, tgt_t, pairs_in, src, tgt, half_s, half_t, real_s, real_t, sum_s, sum_t, tiles, xs, xt, cs, ct, pairs, sems):
     copies = [
         pltpu.make_async_copy(a, b, sems.at[i])
-        for i, (a, b) in enumerate(((counts_s, cs), (src_t, xs), (counts_t, ct), (tgt_t, xt), (pairs_in, pairs_out)))
+        for i, (a, b) in enumerate(((counts_s, cs), (src_t, xs), (counts_t, ct), (tgt_t, xt), (pairs_in, pairs)))
     ]
     for copy in copies:
         copy.start()
@@ -59,6 +60,7 @@
             slot = lane + (row % 2) * LANES
             real[row : row + 1, :] = (slot < counts[row // 2]).astype(jnp.float32)
     copies[4].wait()
+    tiles[...] = pairs[:1, :] * TILE_BASE + pairs[1:, :]
 
 
 def prepare(src_counts, tgt_counts, src_t, tgt_t, pairs):
@@ -77,7 +79,7 @@
             rows_t,
             total,
             total,
-            jax.ShapeDtypeStruct(pairs.shape, jnp.int32),
+            jax.ShapeDtypeStruct((1, pairs.shape[1]), jnp.int32),
             jax.ShapeDtypeStruct(src_t.shape, jnp.bfloat16),
             jax.ShapeDtypeStruct(tgt_t.shape, jnp.bfloat16),
         ),
@@ -86,10 +88,21 @@
         scratch_shapes=[
             pltpu.SMEM(src_counts.shape, jnp.int32),
             pltpu.SMEM(tgt_counts.shape, jnp.int32),
+            pltpu.VMEM(pairs.shape, jnp.int32),
             pltpu.SemaphoreType.DMA((5,)),
         ],
         compiler_params=PARAMS,
     )(*in_hbm(src_counts, tgt_counts, src_t, tgt_t, pairs))
+
+
+def whole(parts_ref, rows):
+    count, height, _ = parts_ref.shape
+    if height >= rows:
+        return merged(parts_ref[:, :rows, :])
+    half = rows // 2
+    return jnp.concatenate(
+        [merged(jnp.stack([parts_ref[i, :half, :] for i in range(c, count, 2)])) for c in (0, 1)], axis=0
+    )
 
 
 def split(value):
@@ -105,14 +118,12 @@
 
 
 def sweep_kernel(
-    side, live_ref, pairs_hbm, parts_ref, red_real, last_ref, col_real, total_ref, red_ref, col_ref,
+    side, live_ref, tiles_ref, parts_ref, red_real, last_ref, col_real, total_ref, red_ref, col_ref,
     out_ref, value_ref, rows, shift, seen, peak, mass, columns, shifts, pairs_ref, sem,
 ):
-    fetch = pltpu.make_async_copy(pairs_hbm, pairs_ref, sem)
-    fetch.start()
     nred = red_ref.shape[0] // BLOCK
     ncol = col_ref.shape[1] // BLOCK
-    value_ref[...] = merged(parts_ref[:, : 2 * nred, :]) if len(parts_ref.shape) == 3 else parts_ref[...]
+    value_ref[...] = whole(parts_ref, 2 * nred) if len(parts_ref.shape) == 3 else parts_ref[...]
     bias = jnp.where(by_block(red_real) > 0.0, -by_block(value_ref), very_low)
     hi, mid, low = split(bias)
     for i in range(nred // PART):
@@ -133,12 +144,12 @@
         shifts[c] = chunk.astype(jnp.bfloat16)
     seen[...] = jnp.zeros(seen.shape, jnp.float32)
     mass[...] = jnp.zeros(mass.shape, jnp.float32)
-    fetch.wait()
     live = live_ref[0, 0]
 
-    def scores(t):
-        red = pairs_ref[side, t]
-        col = pairs_ref[1 - side, t]
+    def scores(t, both):
+        red, col = both & (TILE_BASE - 1), lax.shift_right_logical(both, TILE_BITS)
+        if side == 0:
+            red, col = col, red
         place = lane - (red & (PART - 1))
         ones = ((place == 0) | (place == PART) | (place == 2 * PART)).astype(jnp.float32).astype(jnp.bfloat16)
         ones = jnp.broadcast_to(ones, (3 * PART, BLOCK))
@@ -146,20 +157,20 @@
         rhs = col_ref[:, pl.ds(pl.multiple_of(col * BLOCK, BLOCK), BLOCK)]
         rhs = jnp.concatenate([rhs, ones, shifts[col]], axis=0)
         score = jnp.dot(lhs, rhs, preferred_element_type=jnp.float32)
-        return score.reshape(BLOCK // 8, 8, BLOCK), col, jnp.where(t < live, col, ncol)
+        return score.reshape(BLOCK // 8, 8, BLOCK), jnp.where(t < live, col, ncol)
+
+    tiles = tiles_ref[...]
+
+    own = [tiles[0, t] for t in range(tiles.shape[1])]
 
     def tile(t):
-        score, col, slot = scores(t)
+        score, slot = scores(t, own[t])
         terms = jnp.exp2(score * SCALE)
         mass[slot] = mass[slot] + jnp.sum(terms, axis=0)
         seen[pl.ds(slot, 1), :] = jnp.ones((1, LANES), jnp.float32)
 
-    def group(i, _):
-        for u in range(GROUP):
-            tile(i * GROUP + u)
-        return 0
-
-    lax.fori_loop(0, (live + GROUP - 1) // GROUP, group, 0)
+    for t in range(tiles.shape[1]):
+        tile(t)
 
     def finish(part):
         for h in (0, 1):
@@ -177,11 +188,14 @@
 
     @pl.when(lost > 0.0)
     def _():
+        fetch = pltpu.make_async_copy(tiles_ref, pairs_ref, sem)
+        fetch.start()
+        fetch.wait()
         peak[...] = jnp.full(peak.shape, very_low, jnp.float32)
         mass[...] = jnp.zeros(mass.shape, jnp.float32)
 
         def exact(t, _):
-            score, _, slot = scores(t)
+            score, slot = scores(t, pairs_ref[0, t])
             old = peak[slot]
             new = jnp.maximum(old, jnp.max(score, axis=0))
             terms = jnp.exp2((score - new[None]) * SCALE)
@@ -226,18 +240,23 @@
     )(live, pairs, parts, red_real, last, col_real, total, red, col)
 
 
-def relay_kernel(rows, parts_ref, out_ref):
+def relay_kernel(rows, first, parts_ref, out_ref):
     copies, height, _ = out_ref.shape
-    out_ref[:, :rows, :] = jnp.broadcast_to(merged(parts_ref[:, :rows, :])[None], (copies, rows, LANES))
-    if height > rows:
-        count = jnp.sum(parts_ref[:, rows:, :], axis=0)
-        out_ref[:, rows:, :] = jnp.broadcast_to(count[None], (copies, height - rows, LANES))
-
-
-def relay(rows, copies, parts):
+    start = 0
+    if first:
+        start = pl.multiple_of(lax.axis_index("core") * rows, rows)
+    value = merged(parts_ref[:, pl.ds(start, rows), :])
+    out_ref[:, :rows, :] = jnp.broadcast_to(value[None], (copies, rows, LANES))
+    extra = height - rows
+    if extra:
+        count = jnp.sum(parts_ref[:, parts_ref.shape[1] - extra :, :], axis=0)
+        out_ref[:, rows:, :] = jnp.broadcast_to(count[None], (copies, extra, LANES))
+
+
+def relay(rows, extra, copies, first, parts):
     return pl.pallas_call(
-        functools.partial(relay_kernel, rows),
-        out_shape=jax.ShapeDtypeStruct((copies,) + parts.shape[1:], jnp.float32),
+        functools.partial(relay_kernel, rows, first),
+        out_shape=jax.ShapeDtypeStruct((copies, rows + extra, LANES), jnp.float32),
         in_specs=[VMEM],
         out_specs=VMEM,
         compiler_params=PARAMS,
@@ -247,13 +266,14 @@
 def finish_kernel(
     src_value, src_half, src_real, tgt_parts, tgt_half, tgt_real, first_src, first_tgt, src_out, tgt_out
 ):
+    half = tgt_half.shape[0] // 2
     log_tgt = jnp.log(jnp.sum(first_src[:, src_half.shape[0] :, :], axis=0)[:1])
-    log_src = jnp.log(jnp.sum(first_tgt[:, tgt_half.shape[0] :, :], axis=0)[:1])
+    log_src = jnp.log(sum(first_tgt[i, half:, :] for i in range(0, first_tgt.shape[0], 2))[:1])
     src_shift = -epsilon * (ITERS * log_src - (ITERS - 1) * log_tgt)
     tgt_shift = epsilon * ITERS * (log_src - log_tgt)
     for half, value, shift, real, out in (
         (src_half, src_value[...], src_shift, src_real, src_out),
-        (tgt_half, merged(tgt_parts[...]), tgt_shift, tgt_real, tgt_out),
+        (tgt_half, whole(tgt_parts, tgt_half.shape[0]), tgt_shift, tgt_real, tgt_out),
     ):
         out[...] = jnp.where(real[...] > 0.0, (half[...] - value) * (2.0 / DIM) + shift, 0.0)
 
@@ -289,12 +309,14 @@
             1, out, tile_count, pairs, tgt_parts, tgt_real, src_value, src_real, tgt_total, tgt, src_t
         )
         src_parts = lax.all_to_all(src_parts, "y", 0, 0)
-        out = (sizes["z"], tgt_rows + extra, LANES)
+        out = (1, tgt_rows + extra, LANES)
         tgt_parts, src_value = sweep(
             0, out, tile_count, pairs, src_parts, src_real, tgt_value, tgt_real, src_total, src, tgt_t
         )
+        tgt_parts = lax.all_gather(tgt_parts, "core", axis=0, tiled=True)
+        tgt_parts = relay(tgt_rows // 2, extra, sizes["z"], True, tgt_parts)
         tgt_parts = lax.all_to_all(tgt_parts, "z", 0, 0)
-        tgt_parts = relay(tgt_rows, sizes["x"] * sizes["core"], tgt_parts)
+        tgt_parts = relay(tgt_rows // 2, extra, sizes["x"] * sizes["core"], False, tgt_parts)
         tgt_parts = lax.all_to_all(tgt_parts, ("x", "core"), 0, 0)
         if step == 0:
             first = [src_parts, tgt_parts]

time: 159 us -> 144 us (0.906)
  blocking collectives: 137 us -> 123 us
    all_gather x0 -> x3, blocking collectives: none -> 16.6 us  [on_device(): tgt_parts = lax.all_gather(tgt_parts, 'core', axis=0, tiled=True)]
    all_to_all x3, blocking collectives: 44.6 us -> 29.8 us  [on_device(): tgt_parts = lax.all_to_all(tgt_parts, ('x', 'core'), 0, 0)]
    all_to_all x3, blocking collectives: 50.7 us -> 40.6 us  [on_device(): tgt_parts = lax.all_to_all(tgt_parts, 'z', 0, 0)]
    all_to_all x3, blocking collectives: 41.6 us -> 36.1 us  [on_device(): src_parts = lax.all_to_all(src_parts, 'y', 0, 0)]
where the time goes in v6:
time: 144 us; the launch traced here: 143 us
  blocking collectives  123 us (85%)
  Pallas kernels  18.9 us (13%)
    all_to_all x3, blocking collectives, on_device(): tgt_parts = lax.all_to_all(tgt_parts, 'z', 0, 0)  40.6 us
    all_to_all x3, blocking collectives, on_device(): src_parts = lax.all_to_all(src_parts, 'y', 0, 0)  36.1 us
    all_to_all x3, blocking collectives, on_device(): tgt_parts = lax.all_to_all(tgt_parts, ('x', 'core'), 0, 0)  29.8 us
    all_gather x3, blocking collectives, on_device(): tgt_parts = lax.all_gather(tgt_parts, 'core', axis=0, tiled=True)  16.6 us
    pallas_call x6, Pallas kernels, sweep(): pl.pallas_call(functools.partial(sweep_kernel, side), out_shape=(jax.Shap...  15.9 us

profile of v6, /device:TPU:1, one launch (start us, length us, event | category | flops | bytes accessed | tf_op | source)
XLA Modules:
  0.0 143.5 jit_solution(6561635572695800056)
XLA Ops:
  1.3 2.1 %shard_map.77 = (bf16[4096,128]{1,0:T(8,128)(2,1)S(1)}, bf16[8192,128]{1,0:T(8,128)(2,1)S(1)}, f32[32,128]{1,0:T(8,128)S(1)}, f32[64,128]{1,0:T(8,128)S(1)}, f32...) custom-call(s32[16]{0:T(128)} %counts_s.1, ...), custom_call_target="tpu_custom_call" | custom-call | tf_op jit(solution)/shard_map/pallas_call | solution.py:71
  3.4 2.6 %shard_map.78 = (f32[8,40,128]{2,1,0:T(8,128)S(1)}, f32[64,128]{1,0:T(8,128)S(1)}) custom-call(s32[1,1]{1,0:T(1,128)S(6)} %copy.8.live_ref, s32[1,48]{1,0:T(1,128)S(1)} %get-tuple-element.27.tiles_ref, f32[64,128]{1,0:T(8,128)S(1)} %get-tuple-element.28.parts_ref.tgt_half, f32[64,128]{1,0:T(8,128)S(1)} %get-tuple-element.29.red_real.col_real.tgt_real, ...), custom_call_target="tpu_custom_call" | custom-call | tf_op jit(solution)/shard_map/pallas_call | solution.py:220
  6.0 15.8 %all_to_all.45.parts_ref.first_src = f32[8,40,128]{2,1,0:T(8,128)S(1)} all-to-all(f32[8,40,128]{2,1,0:T(8,128)S(1)} %get-tuple-element.35), channel_id=1, replica_groups=mesh['x'=4,'z'=8,'core'=2,'y'=8] {'y'}, dimensions={0} | all-to-all | bytes 327680 | tf_op jit(solution)/shard_map/all_to_all | solution.py:311
  21.8 2.7 %shard_map.79 = (f32[1,72,128]{2,1,0:T(8,128)S(1)}, f32[32,128]{1,0:T(8,128)S(1)}) custom-call(s32[1,1]{1,0:T(1,128)S(6)} %copy.8.live_ref, s32[1,48]{1,0:T(1,128)S(1)} %get-tuple-element.27.tiles_ref, f32[8,40,128]{2,1,0:T(8,128)S(1)} %all_to_all.45.parts_ref.first_src, f32[32,128]{1,0:T(8,128)S(1)} %get-tuple-element.31.col_real.red_real.src_real, ...), custom_call_target="tpu_custom_call" | custom-call | tf_op jit(solution)/shard_map/pallas_call | solution.py:220
  24.5 9.0 %all_gather.9.parts_ref = f32[2,72,128]{2,1,0:T(8,128)S(1)} all-gather(f32[1,72,128]{2,1,0:T(8,128)S(1)} %get-tuple-element.40), channel_id=1, replica_groups=mesh['x'=4,'z'=8,'core'=2,'y'=8] {'core'}, dimensions={0}, use_global_device_ids=true | all-gather | bytes 110592 | tf_op jit(solution)/shard_map/all_gather | solution.py:316
  33.6 19.0 %all_to_all.46.parts_ref = f32[8,40,128]{2,1,0:T(8,128)S(1)} all-to-all(f32[8,40,128]{2,1,0:T(8,128)S(1)} %shard_map.80), channel_id=1, replica_groups=mesh['x'=4,'z'=8,'core'=2,'y'=8] {'z'}, dimensions={0} | all-to-all | bytes 327680 | tf_op jit(solution)/shard_map/all_to_all | solution.py:318
  52.6 11.4 %all_to_all.47.parts_ref.first_tgt = f32[8,40,128]{2,1,0:T(8,128)S(1)} all-to-all(f32[8,40,128]{2,1,0:T(8,128)S(1)} %shard_map.81), channel_id=1, replica_groups=mesh['x'=4,'z'=8,'core'=2,'y'=8] {'x','core'}, dimensions={0} | all-to-all | bytes 327680 | tf_op jit(solution)/shard_map/all_to_all | solution.py:320
  64.0 2.6 %shard_map.82 = (f32[8,32,128]{2,1,0:T(8,128)S(1)}, f32[64,128]{1,0:T(8,128)S(1)}) custom-call(s32[1,1]{1,0:T(1,128)S(6)} %copy.8.live_ref, s32[1,48]{1,0:T(1,128)S(1)} %get-tuple-element.27.tiles_ref, f32[8,40,128]{2,1,0:T(8,128)S(1)} %all_to_all.47.parts_ref.first_tgt, f32[64,128]{1,0:T(8,128)S(1)} %get-tuple-element.29.red_real.col_real.tgt_real, ...), custom_call_target="tpu_custom_call" | custom-call | tf_op jit(solution)/shard_map/pallas_call | solution.py:220
  66.6 10.2 %all_to_all.48.parts_ref = f32[8,32,128]{2,1,0:T(8,128)S(1)} all-to-all(f32[8,32,128]{2,1,0:T(8,128)S(1)} %get-tuple-element.42), channel_id=1, replica_groups=mesh['x'=4,'z'=8,'core'=2,'y'=8] {'y'}, dimensions={0} | all-to-all | bytes 262144 | tf_op jit(solution)/shard_map/all_to_all | solution.py:311
  76.7 2.7 %shard_map.83 = (f32[1,64,128]{2,1,0:T(8,128)S(1)}, f32[32,128]{1,0:T(8,128)S(1)}) custom-call(s32[1,1]{1,0:T(1,128)S(6)} %copy.8.live_ref, s32[1,48]{1,0:T(1,128)S(1)} %get-tuple-element.27.tiles_ref, f32[8,32,128]{2,1,0:T(8,128)S(1)} %all_to_all.48.parts_ref, f32[32,128]{1,0:T(8,128)S(1)} %get-tuple-element.31.col_real.red_real.src_real, ...), custom_call_target="tpu_custom_call" | custom-call | tf_op jit(solution)/shard_map/pallas_call | solution.py:220
  79.4 3.9 %all_gather.10.parts_ref = f32[2,64,128]{2,1,0:T(8,128)S(1)} all-gather(f32[1,64,128]{2,1,0:T(8,128)S(1)} %get-tuple-element.44), channel_id=1, replica_groups=mesh['x'=4,'z'=8,'core'=2,'y'=8] {'core'}, dimensions={0}, use_global_device_ids=true | all-gather | bytes 98304 | tf_op jit(solution)/shard_map/all_gather | solution.py:316
  83.3 10.8 %all_to_all.49.parts_ref = f32[8,32,128]{2,1,0:T(8,128)S(1)} all-to-all(f32[8,32,128]{2,1,0:T(8,128)S(1)} %shard_map.84), channel_id=1, replica_groups=mesh['x'=4,'z'=8,'core'=2,'y'=8] {'z'}, dimensions={0} | all-to-all | bytes 262144 | tf_op jit(solution)/shard_map/all_to_all | solution.py:318
  94.2 9.2 %all_to_all.50.parts_ref = f32[8,32,128]{2,1,0:T(8,128)S(1)} all-to-all(f32[8,32,128]{2,1,0:T(8,128)S(1)} %shard_map.85), channel_id=1, replica_groups=mesh['x'=4,'z'=8,'core'=2,'y'=8] {'x','core'}, dimensions={0} | all-to-all | bytes 262144 | tf_op jit(solution)/shard_map/all_to_all | solution.py:320
  103.4 2.6 %shard_map.86 = (f32[8,32,128]{2,1,0:T(8,128)S(1)}, f32[64,128]{1,0:T(8,128)S(1)}) custom-call(s32[1,1]{1,0:T(1,128)S(6)} %copy.8.live_ref, s32[1,48]{1,0:T(1,128)S(1)} %get-tuple-element.27.tiles_ref, f32[8,32,128]{2,1,0:T(8,128)S(1)} %all_to_all.50.parts_ref, f32[64,128]{1,0:T(8,128)S(1)} %get-tuple-element.29.red_real.col_real.tgt_real, ...), custom_call_target="tpu_custom_call" | custom-call | tf_op jit(solution)/shard_map/pallas_call | solution.py:220
  106.0 10.1 %all_to_all.51.parts_ref = f32[8,32,128]{2,1,0:T(8,128)S(1)} all-to-all(f32[8,32,128]{2,1,0:T(8,128)S(1)} %get-tuple-element.46), channel_id=1, replica_groups=mesh['x'=4,'z'=8,'core'=2,'y'=8] {'y'}, dimensions={0} | all-to-all | bytes 262144 | tf_op jit(solution)/shard_map/all_to_all | solution.py:311
  116.2 2.7 %shard_map.87 = (f32[1,64,128]{2,1,0:T(8,128)S(1)}, f32[32,128]{1,0:T(8,128)S(1)}) custom-call(s32[1,1]{1,0:T(1,128)S(6)} %copy.8.live_ref, s32[1,48]{1,0:T(1,128)S(1)} %get-tuple-element.27.tiles_ref, f32[8,32,128]{2,1,0:T(8,128)S(1)} %all_to_all.51.parts_ref, f32[32,128]{1,0:T(8,128)S(1)} %get-tuple-element.31.col_real.red_real.src_real, ...), custom_call_target="tpu_custom_call" | custom-call | tf_op jit(solution)/shard_map/pallas_call | solution.py:220
  118.9 3.8 %all_gather.11.parts_ref = f32[2,64,128]{2,1,0:T(8,128)S(1)} all-gather(f32[1,64,128]{2,1,0:T(8,128)S(1)} %get-tuple-element.49), channel_id=1, replica_groups=mesh['x'=4,'z'=8,'core'=2,'y'=8] {'core'}, dimensions={0}, use_global_device_ids=true | all-gather | bytes 98304 | tf_op jit(solution)/shard_map/all_gather | solution.py:316
  122.7 10.8 %all_to_all.52.parts_ref = f32[8,32,128]{2,1,0:T(8,128)S(1)} all-to-all(f32[8,32,128]{2,1,0:T(8,128)S(1)} %shard_map.88), channel_id=1, replica_groups=mesh['x'=4,'z'=8,'core'=2,'y'=8] {'z'}, dimensions={0} | all-to-all | bytes 262144 | tf_op jit(solution)/shard_map/all_to_all | solution.py:318
  133.6 9.2 %all_to_all.53.tgt_parts = f32[8,32,128]{2,1,0:T(8,128)S(1)} all-to-all(f32[8,32,128]{2,1,0:T(8,128)S(1)} %shard_map.89), channel_id=1, replica_groups=mesh['x'=4,'z'=8,'core'=2,'y'=8] {'x','core'}, dimensions={0} | all-to-all | bytes 262144 | tf_op jit(solution)/shard_map/all_to_all | solution.py:320
  142.8 0.7 shard_map.90
  (6 shorter events, 0.2 us)

commit v7 on v6

--- a/solution.py
+++ b/solution.py
@@ -11,7 +11,8 @@
 BLOCK = 256
 ITERS = 3
 LANES = 128
-PART = 16
+PART_BITS = 4
+PART = 1 << PART_BITS
 TILE_BITS = 8
 TILE_BASE = 1 << TILE_BITS
 
@@ -37,13 +38,16 @@
     return top + jnp.log2(total) * INV_SCALE
 
 
-def prepare_kernel(counts_s, counts_t, src_t, tgt_t, pairs_in, src, tgt, half_s, half_t, real_s, real_t, sum_s, sum_t, tiles, xs, xt, cs, ct, pairs, sems):
+def prepare_kernel(live_ref, counts_s, counts_t, src_t, tgt_t, pairs_in, src, tgt, half_s, half_t, real_s, real_t, sum_s, sum_t, must, tiles, hot, xs, xt, cs, ct, pairs, sems):
     copies = [
         pltpu.make_async_copy(a, b, sems.at[i])
         for i, (a, b) in enumerate(((counts_s, cs), (src_t, xs), (counts_t, ct), (tgt_t, xt), (pairs_in, pairs)))
     ]
     for copy in copies:
         copy.start()
+    row = lax.broadcasted_iota(jnp.int32, (3 * PART, BLOCK), 0) & (PART - 1)
+    for block in range(PART):
+        hot[block] = (row == block).astype(jnp.float32).astype(jnp.bfloat16)
     lane = lax.broadcasted_iota(jnp.int32, (1, LANES), 1)
     for side, (counts, points, out, norms, real, total) in enumerate(
         ((cs, xs, src, half_s, real_s, sum_s), (ct, xt, tgt, half_t, real_t, sum_t))
@@ -61,9 +65,17 @@
             real[row : row + 1, :] = (slot < counts[row // 2]).astype(jnp.float32)
     copies[4].wait()
     tiles[...] = pairs[:1, :] * TILE_BASE + pairs[1:, :]
-
-
-def prepare(src_counts, tgt_counts, src_t, tgt_t, pairs):
+    blocks = real_t.shape[0] // 2
+    shape = (blocks, pairs.shape[1])
+    own = pairs[1:, :] == lax.broadcasted_iota(jnp.int32, shape, 0)
+    own = own & (lax.broadcasted_iota(jnp.int32, shape, 1) < live_ref[0, 0])
+    used = jnp.max(jnp.where(own, 1.0, 0.0), axis=1, keepdims=True)
+    for h in (0, 1):
+        half = pl.ds(h, blocks, stride=2)
+        must[half, :] = real_t[half, :] * used
+
+
+def prepare(live, src_counts, tgt_counts, src_t, tgt_t, pairs):
     ns, nt = src_t.shape[1], tgt_t.shape[1]
     rows_s = jax.ShapeDtypeStruct((ns // LANES, LANES), jnp.float32)
     rows_t = jax.ShapeDtypeStruct((nt // LANES, LANES), jnp.float32)
@@ -79,12 +91,14 @@
             rows_t,
             total,
             total,
+            rows_t,
             jax.ShapeDtypeStruct((1, pairs.shape[1]), jnp.int32),
+            jax.ShapeDtypeStruct((PART, 3 * PART, BLOCK), jnp.bfloat16),
             jax.ShapeDtypeStruct(src_t.shape, jnp.bfloat16),
             jax.ShapeDtypeStruct(tgt_t.shape, jnp.bfloat16),
         ),
-        in_specs=[HBM] * 5,
-        out_specs=(VMEM,) * 11,
+        in_specs=[SMEM] + [HBM] * 5,
+        out_specs=(VMEM,) * 13,
         scratch_shapes=[
             pltpu.SMEM(src_counts.shape, jnp.int32),
             pltpu.SMEM(tgt_counts.shape, jnp.int32),
@@ -92,7 +106,7 @@
             pltpu.SemaphoreType.DMA((5,)),
         ],
         compiler_params=PARAMS,
-    )(*in_hbm(src_counts, tgt_counts, src_t, tgt_t, pairs))
+    )(live, *in_hbm(src_counts, tgt_counts, src_t, tgt_t, pairs))
 
 
 def whole(parts_ref, rows):
@@ -118,8 +132,8 @@
 
 
 def sweep_kernel(
-    side, live_ref, tiles_ref, parts_ref, red_real, last_ref, col_real, total_ref, red_ref, col_ref,
-    out_ref, value_ref, rows, shift, seen, peak, mass, columns, shifts, pairs_ref, sem,
+    side, live_ref, tiles_ref, hot_ref, parts_ref, red_real, last_ref, col_real, col_must, total_ref, red_ref, col_ref,
+    out_ref, value_ref, rows, shift, peak, mass, columns, shifts, pairs_ref, sem,
 ):
     nred = red_ref.shape[0] // BLOCK
     ncol = col_ref.shape[1] // BLOCK
@@ -131,7 +145,6 @@
         ones = (lax.broadcasted_iota(jnp.int32, (PART, BLOCK), 0) < 3).astype(jnp.float32)
         pieces = [jnp.zeros((DIM, BLOCK), jnp.float32), hi[own], mid[own], low[own], ones]
         columns[i] = jnp.concatenate(pieces, axis=0).T.astype(jnp.bfloat16)
-    lane = lax.broadcasted_iota(jnp.int32, (3 * PART, 1), 0)
     real = by_block(col_real) > 0.0
     last = jnp.where(real, by_block(last_ref), 0.0)
     shift[...] = last
@@ -142,7 +155,6 @@
         for i in range(3):
             chunk = jnp.where(row == i, lower[i][c : c + 1, :], chunk)
         shifts[c] = chunk.astype(jnp.bfloat16)
-    seen[...] = jnp.zeros(seen.shape, jnp.float32)
     mass[...] = jnp.zeros(mass.shape, jnp.float32)
     live = live_ref[0, 0]
 
@@ -150,12 +162,9 @@
         red, col = both & (TILE_BASE - 1), lax.shift_right_logical(both, TILE_BITS)
         if side == 0:
             red, col = col, red
-        place = lane - (red & (PART - 1))
-        ones = ((place == 0) | (place == PART) | (place == 2 * PART)).astype(jnp.float32).astype(jnp.bfloat16)
-        ones = jnp.broadcast_to(ones, (3 * PART, BLOCK))
-        lhs = red_ref[pl.ds(pl.multiple_of(red * BLOCK, BLOCK), BLOCK), :] + columns[red // PART]
+        lhs = red_ref[pl.ds(pl.multiple_of(red * BLOCK, BLOCK), BLOCK), :] + columns[lax.shift_right_logical(red, PART_BITS)]
         rhs = col_ref[:, pl.ds(pl.multiple_of(col * BLOCK, BLOCK), BLOCK)]
-        rhs = jnp.concatenate([rhs, ones, shifts[col]], axis=0)
+        rhs = jnp.concatenate([rhs, hot_ref[red & (PART - 1)], shifts[col]], axis=0)
         score = jnp.dot(lhs, rhs, preferred_element_type=jnp.float32)
         return score.reshape(BLOCK // 8, 8, BLOCK), jnp.where(t < live, col, ncol)
 
@@ -167,7 +176,6 @@
         score, slot = scores(t, own[t])
         terms = jnp.exp2(score * SCALE)
         mass[slot] = mass[slot] + jnp.sum(terms, axis=0)
-        seen[pl.ds(slot, 1), :] = jnp.ones((1, LANES), jnp.float32)
 
     for t in range(tiles.shape[1]):
         tile(t)
@@ -183,8 +191,7 @@
     total = jnp.sum(mass[:ncol], axis=1)
     good = (total > 1e-27) & (total < 1e30)
     finish(jnp.where(good, shift[...] + jnp.log2(jnp.where(good, total, 1.0)) * INV_SCALE, very_low))
-    used = jnp.concatenate([seen[:ncol, :]] * 2, axis=1) > 0.0
-    lost = jnp.max(jnp.where(used & real & jnp.logical_not(good), 1.0, 0.0))
+    lost = jnp.max(jnp.where(good, 0.0, by_block(col_must)))
 
     @pl.when(lost > 0.0)
     def _():
@@ -215,7 +222,7 @@
         )
 
 
-def sweep(side, out, live, pairs, parts, red_real, last, col_real, total, red, col):
+def sweep(side, out, live, tiles, hot, parts, red_real, last, col_real, col_must, total, red, col):
     nred, ncol = red.shape[0] // BLOCK, col.shape[1] // BLOCK
     return pl.pallas_call(
         functools.partial(sweep_kernel, side),
@@ -223,21 +230,20 @@
             jax.ShapeDtypeStruct(out, jnp.float32),
             jax.ShapeDtypeStruct((2 * nred, LANES), jnp.float32),
         ),
-        in_specs=[SMEM] + [VMEM] * 8,
+        in_specs=[SMEM] + [VMEM] * 10,
         out_specs=(VMEM, VMEM),
         scratch_shapes=[
             pltpu.VMEM((2 * ncol, LANES), jnp.float32),
             pltpu.VMEM((ncol, BLOCK), jnp.float32),
-            pltpu.VMEM((ncol + 8, LANES), jnp.float32),
             pltpu.VMEM((ncol + 1, 8, BLOCK), jnp.float32),
             pltpu.VMEM((ncol + 1, 8, BLOCK), jnp.float32),
             pltpu.VMEM((nred // PART, BLOCK, LANES), jnp.bfloat16),
             pltpu.VMEM((ncol, PART, BLOCK), jnp.bfloat16),
-            pltpu.SMEM(pairs.shape, jnp.int32),
+            pltpu.SMEM(tiles.shape, jnp.int32),
             pltpu.SemaphoreType.DMA,
         ],
         compiler_params=PARAMS,
-    )(live, pairs, parts, red_real, last, col_real, total, red, col)
+    )(live, tiles, hot, parts, red_real, last, col_real, col_must, total, red, col)
 
 
 def relay_kernel(rows, first, parts_ref, out_ref):
@@ -293,8 +299,8 @@
 
 def on_device(sizes, src_points, tgt_points, src_counts, tgt_counts, tile_list, tile_count):
     pairs = tile_list.reshape(tile_list.shape[2:]).T
-    src, tgt, src_half, tgt_half, src_real, tgt_real, src_total, tgt_total, pairs, src_t, tgt_t = prepare(
-        src_counts, tgt_counts, src_points.T, tgt_points.T, pairs
+    src, tgt, src_half, tgt_half, src_real, tgt_real, src_total, tgt_total, must, tiles, hot, src_t, tgt_t = prepare(
+        tile_count, src_counts, tgt_counts, src_points.T, tgt_points.T, pairs
     )
     src_rows = src_half.shape[0]
     tgt_rows = tgt_half.shape[0]
@@ -306,12 +312,12 @@
         extra = src_total.shape[0] if step == 0 else 0
         out = (sizes["y"], src_rows + extra, LANES)
         src_parts, tgt_value = sweep(
-            1, out, tile_count, pairs, tgt_parts, tgt_real, src_value, src_real, tgt_total, tgt, src_t
+            1, out, tile_count, tiles, hot, tgt_parts, tgt_real, src_value, src_real, src_real, tgt_total, tgt, src_t
         )
         src_parts = lax.all_to_all(src_parts, "y", 0, 0)
         out = (1, tgt_rows + extra, LANES)
         tgt_parts, src_value = sweep(
-            0, out, tile_count, pairs, src_parts, src_real, tgt_value, tgt_real, src_total, src, tgt_t
+            0, out, tile_count, tiles, hot, src_parts, src_real, tgt_value, tgt_real, must, src_total, src, tgt_t
         )
         tgt_parts = lax.all_gather(tgt_parts, "core", axis=0, tiled=True)
         tgt_parts = relay(tgt_rows // 2, extra, sizes["z"], True, tgt_parts)

time: 144 us -> 148 us (1.028)
  Pallas kernels: 18.9 us -> 36.3 us
  blocking collectives: 123 us -> 110 us
    pallas_call x6, Pallas kernels: 15.9 us -> 33.2 us  [sweep(): pl.pallas_call(functools.partial(sweep_kernel, side), out_shape=(jax.Shap...]
    all_gather x3, blocking collectives: 16.6 us -> 5.57 us  [on_device(): tgt_parts = lax.all_gather(tgt_parts, 'core', axis=0, tiled=True)]
    all_to_all x3, blocking collectives: 36.1 us -> 34.4 us  [on_device(): src_parts = lax.all_to_all(src_parts, 'y', 0, 0)]
where the time goes in v7:
time: 148 us
  blocking collectives  110 us (74%)
  Pallas kernels  36.3 us (25%)
    all_to_all x3, blocking collectives, on_device(): tgt_parts = lax.all_to_all(tgt_parts, 'z', 0, 0)  41.5 us
    all_to_all x3, blocking collectives, on_device(): src_parts = lax.all_to_all(src_parts, 'y', 0, 0)  34.4 us
    pallas_call x6, Pallas kernels, sweep(): pl.pallas_call(functools.partial(sweep_kernel, side), out_shape=(jax.Shap...  33.2 us
    all_to_all x3, blocking collectives, on_device(): tgt_parts = lax.all_to_all(tgt_parts, ('x', 'core'), 0, 0)  28.7 us
    all_gather x3, blocking collectives, on_device(): tgt_parts = lax.all_gather(tgt_parts, 'core', axis=0, tiled=True)  5.57 us

profile of v7, /device:TPU:1, one launch (start us, length us, event | category | flops | bytes accessed | tf_op | source)
XLA Modules:
  0.0 147.9 jit_solution(10115643964319645608)
XLA Ops:
  1.3 2.2 %shard_map.77 = (bf16[4096,128]{1,0:T(8,128)(2,1)S(1)}, bf16[8192,128]{1,0:T(8,128)(2,1)S(1)}, f32[32,128]{1,0:T(8,128)S(1)}, f32[64,128]{1,0:T(8,128)S(1)}, f32...) custom-call(s32[1,1]{1,0:T(1,128)S(6)} %copy.8.live_ref, ...), custom_call_target="tpu_custom_call" | custom-call | tf_op jit(solution)/shard_map/pallas_call | solution.py:83
  3.5 6.9 %shard_map.78 = (f32[8,40,128]{2,1,0:T(8,128)S(1)}, f32[64,128]{1,0:T(8,128)S(1)}) custom-call(s32[1,1]{1,0:T(1,128)S(6)} %copy.8.live_ref, s32[1,48]{1,0:T(1,128)S(1)} %get-tuple-element.29.tiles_ref, bf16[16,48,256]{2,1,0:T(8,128)(2,1)S(1)} %get-tuple-element.30.hot_ref, f32[64,128]{1,0:T(8,128)S(1)} %get-tuple-element.31.parts_ref.tgt_half, ...), custom_call_target="tpu_custom_call" | custom-call | tf_op jit(solution)/shard_map/pallas_call | solution.py:227
  10.4 11.1 %all_to_all.45.parts_ref.first_src = f32[8,40,128]{2,1,0:T(8,128)S(1)} all-to-all(f32[8,40,128]{2,1,0:T(8,128)S(1)} %get-tuple-element.38), channel_id=1, replica_groups=mesh['x'=4,'z'=8,'core'=2,'y'=8] {'y'}, dimensions={0} | all-to-all | bytes 327680 | tf_op jit(solution)/shard_map/all_to_all | solution.py:317
  21.6 7.1 %shard_map.79 = (f32[1,72,128]{2,1,0:T(8,128)S(1)}, f32[32,128]{1,0:T(8,128)S(1)}) custom-call(s32[1,1]{1,0:T(1,128)S(6)} %copy.8.live_ref, s32[1,48]{1,0:T(1,128)S(1)} %get-tuple-element.29.tiles_ref, bf16[16,48,256]{2,1,0:T(8,128)(2,1)S(1)} %get-tuple-element.30.hot_ref, f32[8,40,128]{2,1,0:T(8,128)S(1)} %all_to_all.45.parts_ref.first_src, ...), custom_call_target="tpu_custom_call" | custom-call | tf_op jit(solution)/shard_map/pallas_call | solution.py:227
  28.7 1.9 %all_gather.9.parts_ref = f32[2,72,128]{2,1,0:T(8,128)S(1)} all-gather(f32[1,72,128]{2,1,0:T(8,128)S(1)} %get-tuple-element.44), channel_id=1, replica_groups=mesh['x'=4,'z'=8,'core'=2,'y'=8] {'core'}, dimensions={0}, use_global_device_ids=true | all-gather | bytes 110592 | tf_op jit(solution)/shard_map/all_gather | solution.py:322
  30.6 19.5 %all_to_all.46.parts_ref = f32[8,40,128]{2,1,0:T(8,128)S(1)} all-to-all(f32[8,40,128]{2,1,0:T(8,128)S(1)} %shard_map.80), channel_id=1, replica_groups=mesh['x'=4,'z'=8,'core'=2,'y'=8] {'z'}, dimensions={0} | all-to-all | bytes 327680 | tf_op jit(solution)/shard_map/all_to_all | solution.py:324
  50.2 10.6 %all_to_all.47.parts_ref.first_tgt = f32[8,40,128]{2,1,0:T(8,128)S(1)} all-to-all(f32[8,40,128]{2,1,0:T(8,128)S(1)} %shard_map.81), channel_id=1, replica_groups=mesh['x'=4,'z'=8,'core'=2,'y'=8] {'x','core'}, dimensions={0} | all-to-all | bytes 327680 | tf_op jit(solution)/shard_map/all_to_all | solution.py:326
  60.7 2.3 %shard_map.82 = (f32[8,32,128]{2,1,0:T(8,128)S(1)}, f32[64,128]{1,0:T(8,128)S(1)}) custom-call(s32[1,1]{1,0:T(1,128)S(6)} %copy.8.live_ref, s32[1,48]{1,0:T(1,128)S(1)} %get-tuple-element.29.tiles_ref, bf16[16,48,256]{2,1,0:T(8,128)(2,1)S(1)} %get-tuple-element.30.hot_ref, f32[8,40,128]{2,1,0:T(8,128)S(1)} %all_to_all.47.parts_ref.first_tgt, ...), custom_call_target="tpu_custom_call" | custom-call | tf_op jit(solution)/shard_map/pallas_call | solution.py:227
  63.1 10.1 %all_to_all.48.parts_ref = f32[8,32,128]{2,1,0:T(8,128)S(1)} all-to-all(f32[8,32,128]{2,1,0:T(8,128)S(1)} %get-tuple-element.46), channel_id=1, replica_groups=mesh['x'=4,'z'=8,'core'=2,'y'=8] {'y'}, dimensions={0} | all-to-all | bytes 262144 | tf_op jit(solution)/shard_map/all_to_all | solution.py:317
  73.2 7.3 %shard_map.83 = (f32[1,64,128]{2,1,0:T(8,128)S(1)}, f32[32,128]{1,0:T(8,128)S(1)}) custom-call(s32[1,1]{1,0:T(1,128)S(6)} %copy.8.live_ref, s32[1,48]{1,0:T(1,128)S(1)} %get-tuple-element.29.tiles_ref, bf16[16,48,256]{2,1,0:T(8,128)(2,1)S(1)} %get-tuple-element.30.hot_ref, f32[8,32,128]{2,1,0:T(8,128)S(1)} %all_to_all.48.parts_ref, ...), custom_call_target="tpu_custom_call" | custom-call | tf_op jit(solution)/shard_map/pallas_call | solution.py:227
  80.6 1.9 %all_gather.10.parts_ref = f32[2,64,128]{2,1,0:T(8,128)S(1)} all-gather(f32[1,64,128]{2,1,0:T(8,128)S(1)} %get-tuple-element.48), channel_id=1, replica_groups=mesh['x'=4,'z'=8,'core'=2,'y'=8] {'core'}, dimensions={0}, use_global_device_ids=true | all-gather | bytes 98304 | tf_op jit(solution)/shard_map/all_gather | solution.py:322
  82.4 11.0 %all_to_all.49.parts_ref = f32[8,32,128]{2,1,0:T(8,128)S(1)} all-to-all(f32[8,32,128]{2,1,0:T(8,128)S(1)} %shard_map.84), channel_id=1, replica_groups=mesh['x'=4,'z'=8,'core'=2,'y'=8] {'z'}, dimensions={0} | all-to-all | bytes 262144 | tf_op jit(solution)/shard_map/all_to_all | solution.py:324
  93.5 9.1 %all_to_all.50.parts_ref = f32[8,32,128]{2,1,0:T(8,128)S(1)} all-to-all(f32[8,32,128]{2,1,0:T(8,128)S(1)} %shard_map.85), channel_id=1, replica_groups=mesh['x'=4,'z'=8,'core'=2,'y'=8] {'x','core'}, dimensions={0} | all-to-all | bytes 262144 | tf_op jit(solution)/shard_map/all_to_all | solution.py:326
  102.6 2.3 %shard_map.86 = (f32[8,32,128]{2,1,0:T(8,128)S(1)}, f32[64,128]{1,0:T(8,128)S(1)}) custom-call(s32[1,1]{1,0:T(1,128)S(6)} %copy.8.live_ref, s32[1,48]{1,0:T(1,128)S(1)} %get-tuple-element.29.tiles_ref, bf16[16,48,256]{2,1,0:T(8,128)(2,1)S(1)} %get-tuple-element.30.hot_ref, f32[8,32,128]{2,1,0:T(8,128)S(1)} %all_to_all.50.parts_ref, ...), custom_call_target="tpu_custom_call" | custom-call | tf_op jit(solution)/shard_map/pallas_call | solution.py:227
  104.9 13.1 %all_to_all.51.parts_ref = f32[8,32,128]{2,1,0:T(8,128)S(1)} all-to-all(f32[8,32,128]{2,1,0:T(8,128)S(1)} %get-tuple-element.50), channel_id=1, replica_groups=mesh['x'=4,'z'=8,'core'=2,'y'=8] {'y'}, dimensions={0} | all-to-all | bytes 262144 | tf_op jit(solution)/shard_map/all_to_all | solution.py:317
  118.0 7.1 %shard_map.87 = (f32[1,64,128]{2,1,0:T(8,128)S(1)}, f32[32,128]{1,0:T(8,128)S(1)}) custom-call(s32[1,1]{1,0:T(1,128)S(6)} %copy.8.live_ref, s32[1,48]{1,0:T(1,128)S(1)} %get-tuple-element.29.tiles_ref, bf16[16,48,256]{2,1,0:T(8,128)(2,1)S(1)} %get-tuple-element.30.hot_ref, f32[8,32,128]{2,1,0:T(8,128)S(1)} %all_to_all.51.parts_ref, ...), custom_call_target="tpu_custom_call" | custom-call | tf_op jit(solution)/shard_map/pallas_call | solution.py:227
  125.2 1.9 %all_gather.11.parts_ref = f32[2,64,128]{2,1,0:T(8,128)S(1)} all-gather(f32[1,64,128]{2,1,0:T(8,128)S(1)} %get-tuple-element.53), channel_id=1, replica_groups=mesh['x'=4,'z'=8,'core'=2,'y'=8] {'core'}, dimensions={0}, use_global_device_ids=true | all-gather | bytes 98304 | tf_op jit(solution)/shard_map/all_gather | solution.py:322
  127.1 11.0 %all_to_all.52.parts_ref = f32[8,32,128]{2,1,0:T(8,128)S(1)} all-to-all(f32[8,32,128]{2,1,0:T(8,128)S(1)} %shard_map.88), channel_id=1, replica_groups=mesh['x'=4,'z'=8,'core'=2,'y'=8] {'z'}, dimensions={0} | all-to-all | bytes 262144 | tf_op jit(solution)/shard_map/all_to_all | solution.py:324
  138.1 9.1 %all_to_all.53.tgt_parts = f32[8,32,128]{2,1,0:T(8,128)S(1)} all-to-all(f32[8,32,128]{2,1,0:T(8,128)S(1)} %shard_map.89), channel_id=1, replica_groups=mesh['x'=4,'z'=8,'core'=2,'y'=8] {'x','core'}, dimensions={0} | all-to-all | bytes 262144 | tf_op jit(solution)/shard_map/all_to_all | solution.py:326
  147.2 0.7 shard_map.90
  (6 shorter events, 0.2 us)
